TPU v7x, 32 devices: a whole 2x2x4 slice. The times are simulated.
32 devices in a mesh: ctx: 8 (over z, core), exp: 4 (over y, x).
Axes of the slice: x: 2, y: 2, z: 4, core: 2. Of those that a mesh axis runs over, the one named last changes fastest.
Arguments:
- grad_out: bfloat16 [4, 1024, 4096], P('exp', 'ctx'), may hold values from -1.796875 to 1.796875
- routes: int32 [4, 1024, 1], P('exp', 'ctx'), may hold values from 0 to 3; in each aligned block of 128 rows (0 to 127, 128 to 255, ..., all dimensions but the last counted through in order) at most 48 rows name the same one
- gate_probs: float32 [4, 1024, 1], P('exp', 'ctx'), may hold values from 0.2 to 1
- saved_pre: bfloat16 [8, 4, 192, 1536], P('ctx', 'exp'), may hold values from -6 to 6
- down_weight: bfloat16 [4, 768, 4096], P('exp', None, 'ctx'), may hold values from -0.21875 to 0.21875
- gate_up_weight: bfloat16 [4, 4096, 1536], P('exp', 'ctx'), may hold values from -0.21875 to 0.21875
- queries: bfloat16 [4, 1024, 4096], P('exp', 'ctx')
- keys_values: bfloat16 [4, 1024, 512], P('exp', 'ctx')
- attn_grad: bfloat16 [4, 1024, 4096], P('exp', 'ctx'), may hold values from -6 to 6
- attn_out: bfloat16 [4, 1024, 4096], P('exp', 'ctx'), may hold values from -6 to 6
Outputs:
- moe_input_grad: bfloat16 [4, 1024, 4096], P('exp', 'ctx')
- prob_grad: bfloat16 [4, 1024, 1], P('exp', 'ctx')
- query_grad: bfloat16 [4, 1024, 4096], P('exp', 'ctx')
- kv_grad: bfloat16 [4, 1024, 512], P('exp', 'ctx')
Inputs may be any that keep to these rules, and one draw needn't show every extreme that they name: `routes`: in the rows of one device no expert is named by more than 48 tokens, a bound that some block reaches.
All inputs are finite; a program needn't handle non-finite values.
Results may differ from a plain program's by a relative error of at most 0.0065.
Values may be sent and summed in bfloat16 or wider, within the bound.
A program may use at most 192 MiB of HBM per device.

v0:
```python
import jax
import jax.numpy as jnp
from jax import lax
from jax.sharding import PartitionSpec as P

KEY_VALUE_HEADS = 2
HEAD_SIZE = 128


def expert_pass(expert_rows, pre_acts, down_shard, gate_up_shard):
    hidden = down_shard.shape[0]
    down_grad = lax.dot_general(
        expert_rows,
        lax.all_gather(down_shard, "ctx", axis=1, tiled=True),
        (((1,), (1,)), ((), ())),
        preferred_element_type=jnp.float32,
    )
    gate_pre = pre_acts[:, :hidden].astype(jnp.float32)
    up_pre = pre_acts[:, hidden:].astype(jnp.float32)
    sigma = jax.nn.sigmoid(gate_pre)
    swish = gate_pre * sigma
    slot_prob = jnp.sum(down_grad * swish * up_pre, axis=-1).astype(jnp.bfloat16)
    gate_part = down_grad * up_pre * sigma * (1.0 + gate_pre * (1.0 - sigma))
    up_part = down_grad * swish
    pre_grad = jnp.concatenate([gate_part, up_part], axis=-1).astype(jnp.bfloat16)
    slot_input = lax.dot_general(
        pre_grad,
        lax.all_gather(gate_up_shard, "ctx", axis=0, tiled=True),
        (((1,), (1,)), ((), ())),
        preferred_element_type=jnp.float32,
    ).astype(jnp.bfloat16)
    return (slot_input, slot_prob)


def attend(query_heads, grad_heads, delta_heads, kv_rows):
    seq_len = query_heads.shape[0]
    head_dim = query_heads.shape[2]
    block_len = seq_len // 4
    scale = head_dim ** (-0.5)
    key_rows = kv_rows[:, :head_dim]
    value_rows = kv_rows[:, head_dim:]
    key_grad = jnp.zeros((seq_len, head_dim), jnp.float32)
    value_grad = jnp.zeros((seq_len, head_dim), jnp.float32)
    query_blocks = []
    for block_id in range(4):
        first = block_id * block_len
        reach = first + block_len
        query_block = query_heads[first:reach]
        grad_block = grad_heads[first:reach]
        delta_block = delta_heads[first:reach]
        key_prefix = key_rows[:reach]
        value_prefix = value_rows[:reach]
        scores = (
            jnp.einsum("qhd,kd->qhk", query_block, key_prefix, preferred_element_type=jnp.float32)
            * scale
        )
        row_pos = first + jnp.arange(block_len)
        col_pos = jnp.arange(reach)
        causal = row_pos[:, None, None] >= col_pos[None, None, :]
        scores = jnp.where(causal, scores, jnp.float32(-1e30))
        highest = jnp.max(scores, axis=-1, keepdims=True)
        expo = jnp.exp(scores - highest)
        probs = expo / jnp.sum(expo, axis=-1, keepdims=True)
        low_probs = probs.astype(jnp.bfloat16)
        value_grad = value_grad.at[:reach].add(
            jnp.einsum("qhk,qhd->kd", low_probs, grad_block, preferred_element_type=jnp.float32)
        )
        prob_part = jnp.einsum(
            "qhd,kd->qhk", grad_block, value_prefix, preferred_element_type=jnp.float32
        )
        score_grad = (probs * (prob_part - delta_block[..., None])).astype(jnp.bfloat16)
        query_blocks.append(
            jnp.einsum("qhk,kd->qhd", score_grad, key_prefix, preferred_element_type=jnp.float32)
            * scale
        )
        key_grad = key_grad.at[:reach].add(
            jnp.einsum("qhk,qhd->kd", score_grad, query_block, preferred_element_type=jnp.float32)
            * scale
        )
    return (jnp.concatenate(query_blocks, axis=0), key_grad, value_grad)


def body(
    grad_out,
    routes,
    gate_probs,
    saved_pre,
    down_weight,
    gate_up_weight,
    queries,
    keys_values,
    attn_grad,
    attn_out,
):
    experts = lax.axis_size("exp")
    contexts = lax.axis_size("ctx")
    tok_rows = grad_out.shape[1]
    width = grad_out.shape[2]
    top_count = routes.shape[2]
    capacity = saved_pre.shape[2] // experts
    route_rows = routes[0]
    one_hot = (
        route_rows.reshape(-1)[:, None] == jnp.arange(experts, dtype=jnp.int32)[None, :]
    ).astype(jnp.int32)
    earlier = jnp.cumsum(one_hot, axis=0) - one_hot
    positions = jnp.sum(earlier * one_hot, axis=-1).reshape(tok_rows, top_count)
    slot_keys = route_rows * capacity + positions
    matches = (
        jnp.arange(experts * capacity, dtype=jnp.int32)[:, None, None] == slot_keys[None, :, :]
    )
    dispatch_matrix = jnp.sum(matches.astype(jnp.int32), axis=-1).astype(jnp.bfloat16)
    send_rows = jnp.dot(dispatch_matrix, grad_out[0], preferred_element_type=jnp.float32).astype(
        jnp.bfloat16
    )
    arrived = lax.all_to_all(
        send_rows.reshape(experts, capacity, width), "exp", split_axis=0, concat_axis=0, tiled=True
    )
    expert_rows = arrived.reshape(experts * capacity, width)
    slot_input, slot_prob = expert_pass(
        expert_rows, saved_pre[0, 0], down_weight[0], gate_up_weight[0]
    )
    returned, returned_prob = (
        lax.all_to_all(
            slot_input.reshape(experts, capacity, width),
            "exp",
            split_axis=0,
            concat_axis=0,
            tiled=True,
        ),
        lax.all_to_all(
            slot_prob.reshape(experts, capacity), "exp", split_axis=0, concat_axis=0, tiled=True
        ),
    )
    flat_back = returned.reshape(experts * capacity, width)
    flat_prob = returned_prob.reshape(experts * capacity)
    picked = flat_back[slot_keys[:, 0]]
    running = gate_probs[0][:, 0, None] * picked.astype(jnp.float32)
    moe_input_grad = running.astype(jnp.bfloat16)[None]
    prob_grad = flat_prob[slot_keys][None]
    head_dim = HEAD_SIZE
    key_value_heads = KEY_VALUE_HEADS
    group_copies = contexts // key_value_heads
    local_query = queries[0].reshape(tok_rows, contexts, -1)
    local_grad = attn_grad[0].reshape(tok_rows, contexts, -1)
    kv_local = keys_values[0].reshape(tok_rows, key_value_heads, 2 * head_dim)
    expanded = jnp.repeat(kv_local, group_copies, axis=1)
    local_out = attn_out[0].reshape(tok_rows, contexts, -1)
    wide_query, wide_grad, wide_out, wide_kv = (
        lax.all_to_all(local_query, "ctx", split_axis=1, concat_axis=0, tiled=True),
        lax.all_to_all(local_grad, "ctx", split_axis=1, concat_axis=0, tiled=True),
        lax.all_to_all(local_out, "ctx", split_axis=1, concat_axis=0, tiled=True),
        lax.all_to_all(expanded, "ctx", split_axis=1, concat_axis=0, tiled=True),
    )
    seq_len = wide_query.shape[0]
    product = wide_grad.astype(jnp.float32) * wide_out.astype(jnp.float32)
    delta_heads = jnp.sum(product.reshape(seq_len, -1, head_dim), axis=-1)
    query_heads = wide_query.reshape(seq_len, -1, head_dim)
    grad_heads = wide_grad.reshape(seq_len, -1, head_dim)
    kv_rows = wide_kv.reshape(seq_len, 2 * head_dim)
    query_part, key_portion, value_portion = attend(query_heads, grad_heads, delta_heads, kv_rows)
    query_low = query_part.astype(jnp.bfloat16).reshape(seq_len, 1, -1)
    returned_query = lax.all_to_all(query_low, "ctx", split_axis=0, concat_axis=1, tiled=True)
    query_grad = returned_query.reshape(tok_rows, -1)[None]
    kv_terms = jnp.concatenate([key_portion, value_portion], axis=-1).reshape(
        seq_len, 1, 2 * head_dim
    )
    returned_kv = lax.all_to_all(kv_terms, "ctx", split_axis=0, concat_axis=1, tiled=True)
    kv_summed = jnp.sum(
        returned_kv.reshape(tok_rows, key_value_heads, group_copies, 2 * head_dim), axis=2
    )
    kv_grad = kv_summed.reshape(tok_rows, key_value_heads * 2 * head_dim).astype(jnp.bfloat16)[None]
    return (moe_input_grad, prob_grad, query_grad, kv_grad)


def solution(mesh):
    placed = (
        P("exp", "ctx", None),
        P("exp", "ctx", None),
        P("exp", "ctx", None),
        P("ctx", "exp", None, None),
        P("exp", None, "ctx"),
        P("exp", "ctx", None),
        P("exp", "ctx", None),
        P("exp", "ctx", None),
        P("exp", "ctx", None),
        P("exp", "ctx", None),
    )
    return jax.shard_map(
        body,
        mesh=mesh,
        in_specs=placed,
        out_specs=(
            P("exp", "ctx", None),
            P("exp", "ctx", None),
            P("exp", "ctx", None),
            P("exp", "ctx", None),
        ),
        check_vma=False,
    )
```

profile of v0, /device:TPU:0, one launch (start us, length us, event | category | flops | bytes accessed | tf_op | source)
XLA Modules:
  0.0 362.3 jit_solution(11853530752883332271)
XLA Ops:
  9.1 1.3 copy.138
  10.4 6.3 %all-to-all-start.3 = ((bf16[128,8,512]{2,0,1:T(8,128)(2,1)}), bf16[128,8,512]{2,0,1:T(8,128)(2,1)S(1)}, u32[]{:S(2)}, u32[]{:S(2)}) async-start(bf16[128,8,512]{2,0,1:T(8,128)(2,1)} %copy.138), calls=%async_computation.3 | async-start | bytes 2097152 | tf_op jit(solution)/shard_map/all_to_all | solution.py:149
  18.4 49.0 %all-to-all-done.3 = bf16[128,8,512]{2,0,1:T(8,128)(2,1)S(1)} async-done(((bf16[128,8,512]{2,0,1:T(8,128)(2,1)}), bf16[128,8,512]{2,0,1:T(8,128)(2,1)S(1)}, u32[]{:S(2)}, u32[]{:S(2)}) %all-to-all-start.3) | async-done | bytes 1048608 | tf_op jit(solution)/shard_map/all_to_all | solution.py:149
  67.4 6.4 %all-to-all-start.5 = ((bf16[128,8,512]{2,0,1:T(8,128)(2,1)}), bf16[128,8,512]{2,0,1:T(8,128)(2,1)S(1)}, u32[]{:S(2)}, u32[]{:S(2)}) async-start(bf16[128,8,512]{2,0,1:T(8,128)(2,1)} %copy.141), calls=%async_computation.5 | async-start | bytes 2097152 | tf_op jit(solution)/shard_map/all_to_all | solution.py:150
  73.9 1.6 copy.198
  76.8 39.6 %all-to-all-done.5 = bf16[128,8,512]{2,0,1:T(8,128)(2,1)S(1)} async-done(((bf16[128,8,512]{2,0,1:T(8,128)(2,1)}), bf16[128,8,512]{2,0,1:T(8,128)(2,1)S(1)}, u32[]{:S(2)}, u32[]{:S(2)}) %all-to-all-start.5) | async-done | bytes 1048608 | tf_op jit(solution)/shard_map/all_to_all | solution.py:150
  116.3 4.2 %all-to-all-start.6 = ((bf16[128,8,512]{2,0,1:T(8,128)(2,1)}), bf16[128,8,512]{2,0,1:T(8,128)(2,1)}, u32[]{:S(2)}, u32[]{:S(2)}) async-start(bf16[128,8,512]{2,0,1:T(8,128)(2,1)} %copy.143), calls=%async_computation.6 | async-start | bytes 2097152 | tf_op jit(solution)/shard_map/all_to_all | solution.py:151
  124.4 1.7 convolution_convert_fusion
  126.1 41.5 %all-to-all-done.6 = bf16[128,8,512]{2,0,1:T(8,128)(2,1)} async-done(((bf16[128,8,512]{2,0,1:T(8,128)(2,1)}), bf16[128,8,512]{2,0,1:T(8,128)(2,1)}, u32[]{:S(2)}, u32[]{:S(2)}) %all-to-all-start.6) | async-done | bytes 1048608 | tf_op jit(solution)/shard_map/all_to_all | solution.py:151
  168.5 8.0 %all-to-all-start.4 = ((bf16[128,8,256]{2,0,1:T(8,128)(2,1)}), bf16[128,8,256]{2,0,1:T(8,128)(2,1)S(1)}, u32[]{:S(2)}, u32[]{:S(2)}) async-start(bf16[128,8,256]{2,0,1:T(8,128)(2,1)} %bitcast.22), calls=%async_computation.4 | async-start | bytes 1048576 | tf_op jit(solution)/shard_map/all_to_all | solution.py:152
  179.5 2.8 fusion.13
  182.3 2.0 reshape.633
  185.5 20.7 %all-to-all-done.4 = bf16[128,8,256]{2,0,1:T(8,128)(2,1)S(1)} async-done(((bf16[128,8,256]{2,0,1:T(8,128)(2,1)}), bf16[128,8,256]{2,0,1:T(8,128)(2,1)S(1)}, u32[]{:S(2)}, u32[]{:S(2)}) %all-to-all-start.4) | async-done | bytes 524320 | tf_op jit(solution)/shard_map/all_to_all | solution.py:152
  206.3 4.6 %all-to-all-start = ((bf16[4,48,4096]{2,1,0:T(8,128)(2,1)}), bf16[4,48,4096]{2,1,0:T(8,128)(2,1)}, u32[]{:S(2)}, u32[]{:S(2)}) async-start(bf16[4,48,4096]{2,1,0:T(8,128)(2,1)} %bitcast.266), calls=%async_computation | async-start | bytes 3145728 | tf_op jit(solution)/shard_map/all_to_all | solution.py:115
  217.4 1.6 convolution_bitcast_fusion.4
  219.1 2.2 fusion.114
  221.3 2.2 fusion.59
  223.5 2.2 multiply_convert_fusion.2
  227.0 3.0 fusion.113
  230.0 2.6 multiply_convert_fusion.1
  234.7 3.7 %fusion.112 = (f32[256,4]{0,1:T(4,128)S(1)}, f32[256,4,1024]{2,0,1:T(8,128)}) fusion(pred[256,1024]{1,0:T(8,128)(4,1)S(1)} %copy-done.18, bf16[256,4,128]{0,2,1:T(8,128)(2,1)S(1)} %copy.166, bf16[1024,256]{1,0:T(8,128)(2,1)S(1)} %bitcast.282), kind=kOutput, calls=%fused_computation.159 | convolution fusion | flops 272630784 | bytes 4984832 | tf_op jit(solution)/shard_map/sub | solution.py:62
  238.5 2.6 fusion.52
  245.6 3.8 %copy.172 = f32[1024,1,256]{2,1,0:T(1,128)} copy(f32[1024,1,256]{0,2,1:T(8,128)} %maximum_bitcast_fusion) | data formatting | bytes 2097152 | tf_op jit(solution)/shard_map/reshape | solution.py:164
  249.5 1.4 fusion.40
  252.0 3.6 all-to-all-start.8
  255.6 2.2 fusion.39
  258.9 1.8 fusion.48
  261.8 1.3 fusion.47
  264.2 4.6 %pad_maximum_fusion = bf16[1024,1,512]{2,1,0:T(2,128)(2,1)S(1)} fusion(bf16[256,1,512]{2,1,0:T(2,128)(2,1)} %copy.160, bf16[256,1,512]{2,1,0:T(2,128)(2,1)} %copy.159, bf16[256,1,512]{2,1,0:T(2,128)(2,1)} %copy.158, bf16[256,1,512]{2,1,0:T(2,128)(2,1)} %copy.157), kind=kLoop, calls=%fused_computation.20 | loop fusion | flops 1572864 | bytes 2097152 | tf_op jit(solution)/shard_map/concatenate | solution.py:80
  269.4 8.0 %reduce.19 = bf16[1024,512]{1,0:T(8,128)(2,1)} reduce(bf16[1024,1,512]{2,1,0:T(2,128)(2,1)S(1)} %pad_maximum_fusion, bf16[]{:T(256)} %broadcast.298), dimensions={1}, to_apply=%pad_maximum_fusion.reduce_sub_computation | reduce | bytes 2097154 | tf_op jit(solution)/shard_map/concatenate | solution.py:80
  277.4 2.7 reshape.635
  280.1 2.1 all-to-all-done.8
  283.1 3.8 %all-to-all-start.7 = ((bf16[8,2,32768]{2,1,0:T(2,128)(2,1)}), bf16[8,2,32768]{2,1,0:T(2,128)(2,1)S(1)}, u32[]{:S(2)}, u32[]{:S(2)}) async-start(bf16[8,2,32768]{2,1,0:T(2,128)(2,1)} %reshape.635), calls=%async_computation.7 | async-start | bytes 2097152 | tf_op jit(solution)/shard_map/all_to_all | solution.py:162
  287.0 5.8 %fusion.69 = (bf16[192]{0:T(256)(128)(2,1)S(1)}, bf16[192,768]{1,0:T(8,128)(2,1)S(1)}, bf16[192,768]{1,0:T(8,128)(2,1)S(1)}) fusion(bf16[192,1536]{1,0:T(8,128)(2,1)S(1)} %bitcast.301, bf16[192,4096]{1,0:T(8,128)(2,1)} %bitcast.6, bf16[1,768,4096]{2,1,0:T(8,128)(2,1)} %all-gather.5.cloned.1.call-done), kind=kOutput, calls=%fused_computation.95 | convolution fusion | flops 1210466048 | bytes 9044352 | tf_op jit(solution)/shard_map/dot_general | solution.py:12
  293.4 20.0 %all-to-all-done.7 = bf16[8,2,32768]{2,1,0:T(2,128)(2,1)S(1)} async-done(((bf16[8,2,32768]{2,1,0:T(2,128)(2,1)}), bf16[8,2,32768]{2,1,0:T(2,128)(2,1)S(1)}, u32[]{:S(2)}, u32[]{:S(2)}) %all-to-all-start.7) | async-done | bytes 1048608 | tf_op jit(solution)/shard_map/all_to_all | solution.py:162
  313.4 4.3 %all-to-all-start.2 = ((bf16[4,1,48]{2,1,0:T(2,128)(2,1)}), bf16[4,1,48]{2,1,0:T(2,128)(2,1)S(1)}, u32[]{:S(2)}, u32[]{:S(2)}) async-start(bf16[4,1,48]{2,1,0:T(2,128)(2,1)} %convert_element_type.166), calls=%async_computation.2 | async-start | bytes 4096 | tf_op jit(solution)/shard_map/all_to_all | solution.py:130
  317.7 10.0 %fusion.8 = bf16[192,4096]{1,0:T(8,128)(2,1)} fusion(bf16[1,4096,1536]{2,1,0:T(8,128)(2,1)} %all-gather.7.cloned.1.call-done, bf16[192,768]{1,0:T(8,128)(2,1)S(1)} %get-tuple-element.125, bf16[192,768]{1,0:T(8,128)(2,1)S(1)} %get-tuple-element.126), kind=kOutput, calls=%fused_computation.10 | convolution fusion | flops 2417885184 | bytes 14745600 | tf_op jit(solution)/shard_map/dot_general | solution.py:26
  327.7 4.2 %all-to-all-start.1 = ((bf16[4,48,4096]{2,1,0:T(8,128)(2,1)}), bf16[4,48,4096]{2,1,0:T(8,128)(2,1)S(1)}, u32[]{:S(2)}, u32[]{:S(2)}) async-start(bf16[4,48,4096]{2,1,0:T(8,128)(2,1)} %bitcast.288), calls=%async_computation.1 | async-start | bytes 3145728 | tf_op jit(solution)/shard_map/all_to_all | solution.py:123
  331.9 2.3 copy.173
  334.2 2.0 reduce_sum.92
  336.9 3.5 reshape.636
  340.4 1.9 copy.190
  342.3 1.3 copy.161
  343.6 2.3 copy.175
  346.0 1.7 gather_fusion.1
  347.7 2.6 all-to-all-done.1
  350.4 2.2 gather_fusion
  352.5 2.5 fusion.14
  (139 shorter events, 35.6 us)
Async XLA Ops:
  7.2 117.2 %copy-start = (bf16[1,128,4096]{2,1,0:T(8,128)(2,1)S(1)}, bf16[1,128,4096]{2,1,0:T(8,128)(2,1)}, u32[]{:S(2)}) copy-start(bf16[1,128,4096]{2,1,0:T(8,128)(2,1)} %param.30) | copy-start | bytes 3145732
  7.2 1.5 copy-start.8
  7.2 279.7 %all-gather.5.cloned.1.call-start = ((), (), s32[]{:S(2)}) async-start(), calls=%async_computation.9 | async-start | bytes 7077888 | tf_op jit(solution)/shard_map/all_gather | solution.py:14
  7.9 309.8 %all-gather.7.cloned.1.call-start = ((), (), s32[]{:S(2)}) async-start(), calls=%async_computation.10 | async-start | bytes 14155776 | tf_op jit(solution)/shard_map/all_gather | solution.py:28
  9.1 7.6 %copy-start.9 = (bf16[1,128,4096]{2,1,0:T(8,128)(2,1)S(1)}, bf16[1,128,4096]{2,1,0:T(8,128)(2,1)}, u32[]{:S(2)}) copy-start(bf16[1,128,4096]{2,1,0:T(8,128)(2,1)} %param.38) | copy-start | bytes 3145732
  10.4 57.0 %all-to-all-start.3 = ((bf16[128,8,512]{2,0,1:T(8,128)(2,1)}), bf16[128,8,512]{2,0,1:T(8,128)(2,1)S(1)}, u32[]{:S(2)}, u32[]{:S(2)}) async-start(bf16[128,8,512]{2,0,1:T(8,128)(2,1)} %copy.138), calls=%async_computation.3 | async-start | bytes 2097152 | tf_op jit(solution)/shard_map/all_to_all | solution.py:149
  67.4 48.9 %all-to-all-start.5 = ((bf16[128,8,512]{2,0,1:T(8,128)(2,1)}), bf16[128,8,512]{2,0,1:T(8,128)(2,1)S(1)}, u32[]{:S(2)}, u32[]{:S(2)}) async-start(bf16[128,8,512]{2,0,1:T(8,128)(2,1)} %copy.141), calls=%async_computation.5 | async-start | bytes 2097152 | tf_op jit(solution)/shard_map/all_to_all | solution.py:150
  75.5 45.1 %copy-start.27 = (s32[1,128,1]{1,2,0:T(1,128)S(1)}, s32[1,128,1]{1,2,0:T(1,128)}, u32[]{:S(2)}) copy-start(s32[1,128,1]{1,2,0:T(1,128)} %param.31) | copy-start | bytes 1540
  75.5 45.2 %copy-start.24 = (bf16[1,128,512]{2,1,0:T(8,128)(2,1)S(1)}, bf16[1,128,512]{2,1,0:T(8,128)(2,1)}, u32[]{:S(2)}) copy-start(bf16[1,128,512]{2,1,0:T(8,128)(2,1)} %param.37) | copy-start | bytes 393220
  116.3 51.3 %all-to-all-start.6 = ((bf16[128,8,512]{2,0,1:T(8,128)(2,1)}), bf16[128,8,512]{2,0,1:T(8,128)(2,1)}, u32[]{:S(2)}, u32[]{:S(2)}) async-start(bf16[128,8,512]{2,0,1:T(8,128)(2,1)} %copy.143), calls=%async_computation.6 | async-start | bytes 2097152 | tf_op jit(solution)/shard_map/all_to_all | solution.py:151
  168.5 37.8 %all-to-all-start.4 = ((bf16[128,8,256]{2,0,1:T(8,128)(2,1)}), bf16[128,8,256]{2,0,1:T(8,128)(2,1)S(1)}, u32[]{:S(2)}, u32[]{:S(2)}) async-start(bf16[128,8,256]{2,0,1:T(8,128)(2,1)} %bitcast.22), calls=%async_computation.4 | async-start | bytes 1048576 | tf_op jit(solution)/shard_map/all_to_all | solution.py:152
  185.4 25.5 %copy-start.26 = (pred[256,256]{0,1:T(8,128)(4,1)S(1)}, pred[256,256]{0,1:T(8,128)(4,1)}, u32[]{:S(2)}) copy-start(pred[256,256]{0,1:T(8,128)(4,1)} %iota_compare_fusion.3) | copy-start | bytes 196612
  206.3 35.6 %copy-start.6 = (bf16[128,8,256]{2,0,1:T(8,128)(2,1)}, bf16[128,8,256]{2,0,1:T(8,128)(2,1)S(1)}, u32[]{:S(2)}) copy-start(bf16[128,8,256]{2,0,1:T(8,128)(2,1)S(1)} %all-to-all-done.4) | copy-start | bytes 1572868
  206.3 6.1 %copy-start.19 = (bf16[256,4,128]{0,2,1:T(8,128)(2,1)S(1)}, bf16[256,4,128]{0,2,1:T(8,128)(2,1)}, u32[]{:S(2)}) copy-start(bf16[256,4,128]{0,2,1:T(8,128)(2,1)} %copy.168) | copy-start | bytes 786436
  206.3 45.7 %all-to-all-start = ((bf16[4,48,4096]{2,1,0:T(8,128)(2,1)}), bf16[4,48,4096]{2,1,0:T(8,128)(2,1)}, u32[]{:S(2)}, u32[]{:S(2)}) async-start(bf16[4,48,4096]{2,1,0:T(8,128)(2,1)} %bitcast.266), calls=%async_computation | async-start | bytes 3145728 | tf_op jit(solution)/shard_map/all_to_all | solution.py:115
  211.4 1.0 copy-start.30
  212.4 1.5 copy-start.14
  212.7 0.8 copy-start.7
  213.5 0.9 copy-start.15
  213.5 2.0 copy-start.12
  213.8 1.9 copy-start.13
  214.0 2.1 copy-start.10
  214.5 1.8 copy-start.11
  215.6 1.8 copy-start.20
  217.4 1.7 copy-start.25
  219.1 2.2 copy-start.22
  223.5 3.5 copy-start.23
  225.7 1.0 copy-start.3
  232.6 1.2 copy-start.2
  233.8 0.9 copy-start.18
  238.5 3.4 copy-start.21
  238.5 3.4 copy-start.31
  241.1 0.8 copy-start.16
  243.0 1.0 copy-start.17
  244.6 4.9 %copy-start.4 = (bf16[256,4,512]{2,0,1:T(8,128)(2,1)S(1)}, bf16[256,4,512]{2,0,1:T(8,128)(2,1)}, u32[]{:S(2)}) copy-start(bf16[256,4,512]{2,0,1:T(8,128)(2,1)} %copy-done.3) | copy-start | bytes 3145732
  252.0 30.1 %all-to-all-start.8 = ((f32[1024,1,256]{2,1,0:T(1,128)}), f32[1024,1,256]{2,1,0:T(1,128)S(1)}, u32[]{:S(2)}, u32[]{:S(2)}) async-start(f32[1024,1,256]{2,1,0:T(1,128)} %copy.172), calls=%async_computation.8 | async-start | bytes 2097152 | tf_op jit(solution)/shard_map/all_to_all | solution.py:167
  277.4 9.6 %copy-start.29 = (bf16[1,1,192,1536]{3,2,1,0:T(8,128)(2,1)S(1)}, bf16[1,1,192,1536]{3,2,1,0:T(8,128)(2,1)}, u32[]{:S(2)}) copy-start(bf16[1,1,192,1536]{3,2,1,0:T(8,128)(2,1)} %param.33) | copy-start | bytes 1769476
  282.1 1.0 copy-start.5
  283.1 30.3 %all-to-all-start.7 = ((bf16[8,2,32768]{2,1,0:T(2,128)(2,1)}), bf16[8,2,32768]{2,1,0:T(2,128)(2,1)S(1)}, u32[]{:S(2)}, u32[]{:S(2)}) async-start(bf16[8,2,32768]{2,1,0:T(2,128)(2,1)} %reshape.635), calls=%async_computation.7 | async-start | bytes 2097152 | tf_op jit(solution)/shard_map/all_to_all | solution.py:162
  313.4 14.2 %all-to-all-start.2 = ((bf16[4,1,48]{2,1,0:T(2,128)(2,1)}), bf16[4,1,48]{2,1,0:T(2,128)(2,1)S(1)}, u32[]{:S(2)}, u32[]{:S(2)}) async-start(bf16[4,1,48]{2,1,0:T(2,128)(2,1)} %convert_element_type.166), calls=%async_computation.2 | async-start | bytes 4096 | tf_op jit(solution)/shard_map/all_to_all | solution.py:130
  327.7 22.7 %all-to-all-start.1 = ((bf16[4,48,4096]{2,1,0:T(8,128)(2,1)}), bf16[4,48,4096]{2,1,0:T(8,128)(2,1)S(1)}, u32[]{:S(2)}, u32[]{:S(2)}) async-start(bf16[4,48,4096]{2,1,0:T(8,128)(2,1)} %bitcast.288), calls=%async_computation.1 | async-start | bytes 3145728 | tf_op jit(solution)/shard_map/all_to_all | solution.py:123
  350.4 2.2 copy-start.28
  350.4 4.6 %copy-start.1 = (bf16[1,128,4096]{2,1,0:T(8,128)(2,1)S(1)}, bf16[1,128,4096]{2,1,0:T(8,128)(2,1)}, u32[]{:S(2)}) copy-start(bf16[1,128,4096]{2,1,0:T(8,128)(2,1)} %param.30) | copy-start | bytes 3145732
Sparse Core Ops, SparseCore 0:
  9.6 107.7 all-gather.4
  119.1 142.3 all-gather.6
where the time goes:
time: 369 us; the launch traced here: 362 us
  waiting for transfers between devices  177 us (48%)
  local copies, waits for them, and re-layouts  50.7 us (14%)
  matrix products  48.1 us (13%)
  starting transfers between devices  45.5 us (12%)
  other arithmetic  25.8 us (7%)
  between operations  15.1 us (4%)
    all_to_all x1, waiting for transfers between devices, body(): lax.all_to_all(local_query, 'ctx', split_axis=1, concat_axis=0, tiled=True)  49 us
    all_to_all x1, waiting for transfers between devices, body(): lax.all_to_all(local_out, 'ctx', split_axis=1, concat_axis=0, tiled=True)  41.5 us
    all_to_all x1, waiting for transfers between devices, body(): lax.all_to_all(local_grad, 'ctx', split_axis=1, concat_axis=0, tiled=True)  39.6 us
    unnamed x76, local copies, waits for them, and re-layouts  21 us
    all_to_all x1, waiting for transfers between devices, body(): lax.all_to_all(expanded, 'ctx', split_axis=1, concat_axis=0, tiled=True)  20.7 us
    all_to_all x1, waiting for transfers between devices, body(): lax.all_to_all(query_low, 'ctx', split_axis=0, concat_axis=1, tiled=True)  20 us
    concatenate x2, other arithmetic, attend(): return (jnp.concatenate(query_blocks, axis=0), key_grad, value_grad)  12.6 us
    dot_general x1, matrix products, expert_pass(): lax.dot_general(pre_grad, lax.all_gather(gate_up_shard, 'ctx', axis=0, ti...  9.97 us
  transfers between devices with their start and end apart: 11, of which 7 were waited for; matrix products, arithmetic and copies ran while one was open for 31% of the time, Pallas kernels for 0%

commit v1 on v0

v1 whole, which is shorter than its diff:
```python
import functools

import jax
import jax.numpy as jnp
from jax import lax
from jax.experimental import pallas as pl
from jax.experimental.pallas import tpu as pltpu
from jax.sharding import PartitionSpec as P

KEY_VALUE_HEADS = 2
HEAD_SIZE = 128
LOG2E = 1.4426950408889634
NT = (((1,), (1,)), ((), ()))


def attention_kernel(
    pairs, pos_ref, q_ref, g_ref, o_ref, kv_ref, dq_ref, dkv_ref, kt_ref, bias_ref, st_ref, ds_ref
):
    seq_len = kv_ref.shape[0]
    rows = q_ref.shape[0]
    hd = HEAD_SIZE
    scale = hd**-0.5
    chunk = 256
    chunks = [pl.ds(i * chunk, chunk) for i in range(seq_len // chunk)]

    @pl.when(pl.program_id(1) == 0)
    def _():
        kt_ref[...] = kv_ref[:, :hd].astype(jnp.float32).T.astype(jnp.bfloat16)
        dkv_ref[...] = jnp.zeros_like(dkv_ref)
        key_pos = lax.broadcasted_iota(jnp.int32, bias_ref.shape, 0)
        row_pos = pos_ref[0] + lax.broadcasted_iota(jnp.int32, bias_ref.shape, 1) % rows
        bias_ref[...] = jnp.where(key_pos <= row_pos, 0.0, -1e30).astype(jnp.float32)

    for pair in range(pairs):
        cols = [pl.ds((2 * pair + i) * hd, hd) for i in range(2)]
        q2 = jnp.concatenate([q_ref[:, col] for col in cols], axis=0)
        g2 = jnp.concatenate([g_ref[:, col] for col in cols], axis=0)
        o2 = jnp.concatenate([o_ref[:, col] for col in cols], axis=0)
        prod = g2.astype(jnp.float32) * o2.astype(jnp.float32)
        delta = jnp.sum(prod.T, axis=0, keepdims=True)
        top = jnp.full((1, 2 * rows), -jnp.inf, jnp.float32)
        for part in chunks:
            s = lax.dot_general(kv_ref[part, :hd], q2, NT, preferred_element_type=jnp.float32)
            s = s + bias_ref[part, :]
            st_ref[pair, part, :] = s
            top = jnp.maximum(top, jnp.max(s, axis=0, keepdims=True))
        total = jnp.zeros((1, 2 * rows), jnp.float32)
        for part in chunks:
            e = jnp.exp2((st_ref[pair, part, :] - top) * (scale * LOG2E))
            st_ref[pair, part, :] = e
            total = total + jnp.sum(e, axis=0, keepdims=True)
        inverse = 1.0 / total
        for part in chunks:
            p = st_ref[pair, part, :] * inverse
            dkv_ref[part, hd:] += jnp.dot(
                p.astype(jnp.bfloat16), g2, preferred_element_type=jnp.float32
            )
            dp = lax.dot_general(kv_ref[part, hd:], g2, NT, preferred_element_type=jnp.float32)
            ds = (p * (dp - delta)).astype(jnp.bfloat16)
            ds_ref[pair, part, :] = ds
            dkv_ref[part, :hd] += jnp.dot(ds, q2, preferred_element_type=jnp.float32) * scale
        dqt = jnp.dot(kt_ref[...], ds_ref[pair], preferred_element_type=jnp.float32) * scale
        dq = dqt.T
        for i in range(2):
            dq_ref[:, cols[i]] = dq[i * rows : (i + 1) * rows].astype(dq_ref.dtype)


def attention(q, g, o, kv, first):
    rows, width = q.shape
    seq_len = kv.shape[0]
    hd = HEAD_SIZE
    pairs = 2
    step = pairs * 2 * hd
    steps = width // KEY_VALUE_HEADS // step
    tok = pl.BlockSpec((rows, step), lambda h, i: (0, h * steps + i))
    key = pl.BlockSpec((seq_len, 2 * hd), lambda h, i: (0, h))
    return pl.pallas_call(
        functools.partial(attention_kernel, pairs),
        grid=(KEY_VALUE_HEADS, steps),
        in_specs=[pl.BlockSpec(memory_space=pltpu.SMEM), tok, tok, tok, key],
        out_specs=[tok, key],
        out_shape=[
            jax.ShapeDtypeStruct((rows, width), jnp.bfloat16),
            jax.ShapeDtypeStruct((seq_len, kv.shape[1]), jnp.float32),
        ],
        scratch_shapes=[
            pltpu.VMEM((hd, seq_len), jnp.bfloat16),
            pltpu.VMEM((seq_len, 2 * rows), jnp.float32),
            pltpu.VMEM((pairs, seq_len, 2 * rows), jnp.float32),
            pltpu.VMEM((pairs, seq_len, 2 * rows), jnp.bfloat16),
        ],
        compiler_params=pltpu.CompilerParams(vmem_limit_bytes=40 * 1024 * 1024),
        cost_estimate=pl.CostEstimate(
            flops=10 * rows * seq_len * width,
            bytes_accessed=8 * rows * width + 6 * seq_len * kv.shape[1],
            transcendentals=rows * seq_len * width // hd,
        ),
    )(first, q, g, o, kv)


def body(
    grad_out,
    routes,
    gate_probs,
    saved_pre,
    down_weight,
    gate_up_weight,
    queries,
    keys_values,
    attn_grad,
    attn_out,
):
    experts = lax.axis_size("exp")
    contexts = lax.axis_size("ctx")
    tok_rows = grad_out.shape[1]
    width = grad_out.shape[2]
    capacity = saved_pre.shape[2] // experts
    hidden = down_weight.shape[1]
    chips = contexts // 2
    pair_groups = [[2 * i, 2 * i + 1] for i in range(chips)]
    chip_groups = [[2 * i + core for i in range(chips)] for core in range(2)]

    kv_all = lax.all_gather(keys_values[0], "ctx", axis=0, tiled=True)
    down_full = lax.all_gather(down_weight[0], "ctx", axis=1, tiled=True)
    gate_up = lax.all_gather(
        gate_up_weight[0], "ctx", axis=0, tiled=True, axis_index_groups=pair_groups
    )

    route_rows = routes[0]
    one_hot = (
        route_rows.reshape(-1)[:, None] == jnp.arange(experts, dtype=jnp.int32)[None, :]
    ).astype(jnp.int32)
    earlier = jnp.cumsum(one_hot, axis=0) - one_hot
    positions = jnp.sum(earlier * one_hot, axis=-1)
    slot_keys = route_rows[:, 0] * capacity + positions
    slots = experts * capacity
    dispatch = (jnp.arange(slots, dtype=jnp.int32)[:, None] == slot_keys[None, :]).astype(
        jnp.bfloat16
    )
    send_rows = jnp.dot(dispatch, grad_out[0], preferred_element_type=jnp.float32).astype(
        jnp.bfloat16
    )
    expert_rows = lax.all_to_all(
        send_rows.reshape(experts, capacity, width), "exp", split_axis=0, concat_axis=0, tiled=True
    ).reshape(slots, width)

    first = (lax.axis_index("ctx") * tok_rows).astype(jnp.int32).reshape(1)
    query_grad, kv_terms = attention(queries[0], attn_grad[0], attn_out[0], kv_all, first)
    kv_grad = lax.psum_scatter(kv_terms, "ctx", scatter_dimension=0, tiled=True).astype(
        jnp.bfloat16
    )

    down_grad = lax.dot_general(expert_rows, down_full, NT, preferred_element_type=jnp.float32)
    pre_acts = saved_pre[0, 0]
    gate_pre = pre_acts[:, :hidden].astype(jnp.float32)
    up_pre = pre_acts[:, hidden:].astype(jnp.float32)
    sigma = jax.nn.sigmoid(gate_pre)
    swish = gate_pre * sigma
    slot_prob = jnp.sum(down_grad * swish * up_pre, axis=-1).astype(jnp.bfloat16)
    gate_part = down_grad * up_pre * sigma * (1.0 + gate_pre * (1.0 - sigma))
    up_part = down_grad * swish
    pre_grad = jnp.concatenate([gate_part, up_part], axis=-1).astype(jnp.bfloat16)

    pre_all = lax.all_gather(pre_grad, "ctx", axis=0, tiled=True, axis_index_groups=chip_groups)
    slot_input = lax.dot_general(pre_all, gate_up, NT, preferred_element_type=jnp.float32).astype(
        jnp.bfloat16
    )
    columns = slot_input.shape[1]
    back = lax.all_to_all(
        slot_input.reshape(chips, experts, capacity, columns),
        "exp",
        split_axis=1,
        concat_axis=1,
        tiled=True,
    ).reshape(chips, slots, columns)
    keys_all, gates_all = (
        lax.all_gather(item, "ctx", axis=0, axis_index_groups=chip_groups)
        for item in (slot_keys, gate_probs[0, :, 0])
    )
    pick = (keys_all[:, :, None] == jnp.arange(slots, dtype=jnp.int32)).astype(jnp.bfloat16)
    picked = jnp.einsum("cts,csd->ctd", pick, back, preferred_element_type=jnp.float32)
    combined = (gates_all[:, :, None] * picked).astype(jnp.bfloat16)
    returned = lax.all_to_all(
        combined, "ctx", split_axis=0, concat_axis=0, tiled=True, axis_index_groups=chip_groups
    )
    moe_input_grad = returned.transpose(1, 0, 2).reshape(1, tok_rows, width)
    back_prob = lax.all_to_all(
        slot_prob.reshape(experts, capacity), "exp", split_axis=0, concat_axis=0, tiled=True
    ).reshape(slots)
    prob_grad = back_prob[slot_keys][None, :, None]
    return (moe_input_grad, prob_grad, query_grad[None], kv_grad[None])


def solution(mesh):
    tok = P("exp", "ctx", None)
    placed = (
        tok,
        tok,
        tok,
        P("ctx", "exp", None, None),
        P("exp", None, "ctx"),
        tok,
        tok,
        tok,
        tok,
        tok,
    )
    return jax.shard_map(
        body,
        mesh=mesh,
        in_specs=placed,
        out_specs=(tok, tok, tok, tok),
        check_vma=False,
    )
```

time: 369 us -> 241 us (0.65); the launches traced: 362 us -> 241 us
  waiting for transfers between devices: 177 us -> 125 us
  local copies, waits for them, and re-layouts: 50.7 us -> 8.48 us
  blocking collectives: 0 us -> 42 us
  matrix products: 48.1 us -> 13.2 us
  starting transfers between devices: 45.5 us -> 10.7 us
  Pallas kernels: 0 us -> 24.3 us
  other arithmetic: 25.8 us -> 2.95 us
    all_to_all x8 -> x2, waiting for transfers between devices: 176 us -> 22.5 us  [the longest x1 21 us: body(): lax.all_to_all(combined, 'ctx', split_axis=0, concat_axis=0, tiled=True,...]
    all_gather x2 -> x4, waiting for transfers between devices: 0.02 us -> 97.5 us  [the longest x1 41.8 us: body(): down_full = lax.all_gather(down_weight[0], 'ctx', axis=1, tiled=True)]
    all_to_all x8 -> x2, starting transfers between devices: 41.2 us -> 7.3 us  [the longest x1 3.78 us: body(): lax.all_to_all(slot_input.reshape(chips, experts, capacity, columns), 'ex...]
    dot_general x19 -> x4, matrix products: 38.7 us -> 13.2 us  [the longest x1 5.95 us: body(): lax.dot_general(expert_rows, down_full, NT, preferred_element_type=jnp.fl...]
    all_to_all x0 -> x1, blocking collectives: none -> 24.8 us  [body(): lax.all_to_all(send_rows.reshape(experts, capacity, width), 'exp', split_...]
    pallas_call x0 -> x1, Pallas kernels: none -> 24.3 us  [attention(): pl.pallas_call(functools.partial(attention_kernel, pairs), grid=(KEY_VALU...]
    all_gather x0 -> x2, blocking collectives: none -> 17.2 us  [body(): lax.all_gather(item, 'ctx', axis=0, axis_index_groups=chip_groups)]
    unnamed x76 -> x15, local copies, waits for them, and re-layouts: 21 us -> 3.79 us
  transfers between devices with their start and end apart: 11 -> 8, of which waited for: 7 -> 6; matrix products, arithmetic and copies ran while one was open for 31% -> 8% of each run, Pallas kernels for 0% -> 10%
where the time goes in v1:
time: 241 us
  waiting for transfers between devices  125 us (52%)
  blocking collectives  42 us (17%)
  Pallas kernels  24.3 us (10%)
  between operations  13.9 us (6%)
  matrix products  13.2 us (5%)
  starting transfers between devices  10.7 us (4%)
  local copies, waits for them, and re-layouts  8.48 us (4%)
  other arithmetic  2.95 us (1%)
    all_gather x1, waiting for transfers between devices, body(): down_full = lax.all_gather(down_weight[0], 'ctx', axis=1, tiled=True)  41.8 us
    all_gather x1, waiting for transfers between devices, body(): lax.all_gather(pre_grad, 'ctx', axis=0, tiled=True, axis_index_groups=chi...  40.2 us
    all_to_all x1, blocking collectives, body(): lax.all_to_all(send_rows.reshape(experts, capacity, width), 'exp', split_...  24.8 us
    pallas_call x1, Pallas kernels, attention(): pl.pallas_call(functools.partial(attention_kernel, pairs), grid=(KEY_VALU...  24.3 us
    all_to_all x1, waiting for transfers between devices, body(): lax.all_to_all(combined, 'ctx', split_axis=0, concat_axis=0, tiled=True,...  21 us
    all_gather x2, blocking collectives, body(): lax.all_gather(item, 'ctx', axis=0, axis_index_groups=chip_groups)  17.2 us
    all_gather x1, waiting for transfers between devices, body(): kv_all = lax.all_gather(keys_values[0], 'ctx', axis=0, tiled=True)  15.6 us
    dot_general x1, matrix products, body(): lax.dot_general(expert_rows, down_full, NT, preferred_element_type=jnp.fl...  5.95 us
  transfers between devices with their start and end apart: 8, of which 6 were waited for; matrix products, arithmetic and copies ran while one was open for 8% of the time, Pallas kernels for 10%

profile of v1, /device:TPU:0, one launch (start us, length us, event | category | flops | bytes accessed | tf_op | source)
XLA Modules:
  0.0 240.6 jit_solution(11774406847474020584)
XLA Ops:
  7.2 0.0 copy-start
  7.2 0.0 copy-start.5
  7.2 0.0 all-gather.12.cloned.1.call-start
  7.2 0.7 all-gather.12.cloned.1.call-update
  7.9 0.0 all-gather.16.cloned.1.call-start
  8.0 0.7 all-gather.16.cloned.1.call-update
  8.7 0.0 all-gather.14.cloned.1.call-start
  8.7 0.7 all-gather.14.cloned.1.call-update
  9.4 0.0 all-gather.10.cloned.1.call-start
  9.5 0.0 copy-done.5
  9.5 0.1 fusion.18
  9.6 0.2 reduce_window_sum.11
  9.7 0.2 select_reduce_fusion
  9.9 0.0 copy-done
  9.9 0.6 convolution_convert_fusion
  10.5 24.8 %all_to_all.21 = bf16[4,48,4096]{2,1,0:T(8,128)(2,1)} all-to-all(bf16[4,48,4096]{2,1,0:T(8,128)(2,1)S(1)} %bitcast.57), channel_id=1, replica_groups=mesh['ctx'=8,'exp'=4] {'exp'}, dimensions={0} | all-to-all | bytes 3145728 | tf_op jit(solution)/shard_map/all_to_all | solution.py:143
  35.3 41.8 %all-gather.12.cloned.1.call-done = bf16[1,768,4096]{2,1,0:T(8,128)(2,1)} async-done(((bf16[1,768,512]{2,1,0:T(8,128)(2,1)}), bf16[1,768,4096]{2,1,0:T(8,128)(2,1)}) %all-gather.12.cloned.1.call-update) | async-done | bytes 6291472 | tf_op jit(solution)/shard_map/all_gather | solution.py:124
  77.1 6.0 %fusion.11 = (bf16[192]{0:T(256)(128)(2,1)S(1)}, bf16[192,768]{1,0:T(8,128)(2,1)S(1)}, bf16[192,768]{1,0:T(8,128)(2,1)S(1)}) fusion(bf16[192,1536]{1,0:T(8,128)(2,1)} %bitcast.67, bf16[192,4096]{1,0:T(8,128)(2,1)} %bitcast.60, bf16[1,768,4096]{2,1,0:T(8,128)(2,1)} %all-gather.12.cloned.1.call-done), kind=kOutput, calls=%fused_computation.17 | convolution fusion | flops 1210466048 | bytes 9044352 | tf_op jit(solution)/shard_map/dot_general | solution.py:153
  83.0 0.9 pad_maximum_fusion
  83.9 0.0 all-gather.10.cloned.1.call-update
  83.9 0.0 reduce-scatter.2.cloned.1.call-start
  84.0 15.6 %all-gather.16.cloned.1.call-done = bf16[1,1024,512]{2,1,0:T(8,128)(2,1)} async-done(((bf16[1,128,512]{2,1,0:T(8,128)(2,1)}), bf16[1,1024,512]{2,1,0:T(8,128)(2,1)}) %all-gather.16.cloned.1.call-update) | async-done | bytes 1048592 | tf_op jit(solution)/shard_map/all_gather | solution.py:123
  99.5 0.0 copy-done.1
  99.5 1.2 copy-done.3
  100.8 1.2 copy-done.4
  102.0 24.3 %shard_map.129 = (bf16[128,4096]{1,0:T(8,128)(2,1)}, f32[1024,512]{1,0:T(8,128)}) custom-call(s32[1]{0:T(128)} %bitcast.20.pos_ref, bf16[128,4096]{1,0:T(8,128)(2,1)S(1)} %bitcast.52, bf16[128,4096]{1,0:T(8,128)(2,1)S(1)} %bitcast.53, bf16[128,4096]{1,0:T(8,128)(2,1)S(1)} %bitcast.54, bf16[1024,512]{1,0:T(8,128)(2,1)S(1)} %bitcast.55), custom_call_target="tpu_custom_call" | custom-call | flops 5368709120 | bytes 7340032 | tf_op jit(solution)/shard_map/pallas_call | solution.py:77
  126.3 0.0 reduce-scatter.2.cloned.1.call-update
  126.3 0.0 all-gather.14.cloned.1.call-done
  126.3 40.2 %all-gather.10.cloned.1.call-done = bf16[768,1536]{1,0:T(8,128)(2,1)} async-done(((bf16[192,1536]{1,0:T(8,128)(2,1)}), bf16[768,1536]{1,0:T(8,128)(2,1)}) %all-gather.10.cloned.1.call-update) | async-done | bytes 2359312 | tf_op jit(solution)/shard_map/all_gather | solution.py:164
  166.5 5.2 %fusion.4 = bf16[768,1024]{1,0:T(8,128)(2,1)S(1)} fusion(bf16[768,1536]{1,0:T(8,128)(2,1)} %all-gather.10.cloned.1.call-done, bf16[1,1024,1536]{2,1,0:T(8,128)(2,1)} %all-gather.14.cloned.1.call-done), kind=kOutput, calls=%fused_computation.7 | convolution fusion | flops 2416705536 | bytes 7077888 | tf_op jit(solution)/shard_map/dot_general | solution.py:165
  171.8 1.4 copy.16
  173.1 3.8 %all-to-all-start.1 = ((bf16[4,4,48,1024]{3,2,0,1:T(8,128)(2,1)}), bf16[4,4,48,1024]{3,2,0,1:T(8,128)(2,1)S(1)}, u32[]{:S(2)}, u32[]{:S(2)}) async-start(bf16[4,4,48,1024]{3,2,0,1:T(8,128)(2,1)} %copy.16), calls=%async_computation.1 | async-start | bytes 3145728 | tf_op jit(solution)/shard_map/all_to_all | solution.py:169
  176.9 8.6 %all-gather.4 = s32[4,1,128]{2,1,0:T(1,128)S(1)} all-gather(s32[1,1,128]{2,1,0:T(1,128)S(1)} %fusion.21), channel_id=1, replica_groups={{0,8,16,24},{4,12,20,28},{1,9,17,25},{5,13,21,29},{2,10,18,26},{6,14,22..., dimensions={0}, use_global_device_ids=true | all-gather | bytes 2560 | tf_op jit(solution)/shard_map/all_gather | solution.py:177
  185.5 8.6 %all-gather = f32[4,128,1]{1,2,0:T(1,128)S(1)} all-gather(f32[1,128,1]{1,2,0:T(1,128)S(1)} %copy-done.6), channel_id=2, replica_groups={{0,8,16,24},{4,12,20,28},{1,9,17,25},{5,13,21,29},{2,10,18,26},{6,14,22..., dimensions={0}, use_global_device_ids=true | all-gather | bytes 2560 | tf_op jit(solution)/shard_map/all_gather | solution.py:177
  194.1 0.7 convert_element_type.47
  194.7 1.5 all-to-all-done.1
  196.3 3.2 %all-to-all-start.3 = ((bf16[4,1,48]{2,1,0:T(2,128)(2,1)}), bf16[4,1,48]{2,1,0:T(2,128)(2,1)S(1)}, u32[]{:S(2)}, u32[]{:S(2)}) async-start(bf16[4,1,48]{2,1,0:T(2,128)(2,1)} %convert_element_type.47), calls=%async_computation.3 | async-start | bytes 4096 | tf_op jit(solution)/shard_map/all_to_all | solution.py:187
  199.5 0.2 copy.17
  199.7 1.5 multiply_convert_fusion
  201.2 2.9 %all-to-all-done.3 = bf16[4,1,48]{2,1,0:T(2,128)(2,1)S(1)} async-done(((bf16[4,1,48]{2,1,0:T(2,128)(2,1)}), bf16[4,1,48]{2,1,0:T(2,128)(2,1)S(1)}, u32[]{:S(2)}, u32[]{:S(2)}) %all-to-all-start.3) | async-done | bytes 416 | tf_op jit(solution)/shard_map/all_to_all | solution.py:187
  204.0 3.5 %all-to-all-start.2 = ((bf16[4,128,1024]{2,1,0:T(8,128)(2,1)}), bf16[4,128,1024]{2,1,0:T(8,128)(2,1)S(1)}, u32[]{:S(2)}, u32[]{:S(2)}) async-start(bf16[4,128,1024]{2,1,0:T(8,128)(2,1)} %multiply_convert_fusion), calls=%async_computation.2 | async-start | bytes 2097152 | tf_op jit(solution)/shard_map/all_to_all | solution.py:183
  207.6 0.0 reduce-scatter.2.cloned.1.call-done
  207.6 1.6 convert_bitcast_fusion
  209.3 0.1 reshape.101
  209.3 1.7 gather_fusion
  211.1 21.0 %all-to-all-done.2 = bf16[4,128,1024]{2,1,0:T(8,128)(2,1)S(1)} async-done(((bf16[4,128,1024]{2,1,0:T(8,128)(2,1)}), bf16[4,128,1024]{2,1,0:T(8,128)(2,1)S(1)}, u32[]{:S(2)}, u32[]{:S(2)}) %all-to-all-start.2) | async-done | bytes 1048608 | tf_op jit(solution)/shard_map/all_to_all | solution.py:183
  232.1 0.7 copy.18
  232.8 1.3 copy.20
  (12 shorter events, 0.1 us)
Async XLA Ops:
  7.2 2.8 %copy-start = (bf16[1,128,4096]{2,1,0:T(8,128)(2,1)S(1)}, bf16[1,128,4096]{2,1,0:T(8,128)(2,1)}, u32[]{:S(2)}) copy-start(bf16[1,128,4096]{2,1,0:T(8,128)(2,1)} %param.10) | copy-start | bytes 3145732
  7.2 2.3 copy-start.5
  7.2 69.9 %all-gather.12.cloned.1.call-start = ((), (), s32[]{:S(2)}) async-start(), calls=%async_computation.7 | async-start | bytes 7077888 | tf_op jit(solution)/shard_map/all_gather | solution.py:124
  7.9 91.6 %all-gather.16.cloned.1.call-start = ((), (), s32[]{:S(2)}) async-start(), calls=%async_computation.9 | async-start | bytes 1179648 | tf_op jit(solution)/shard_map/all_gather | solution.py:123
  8.7 117.6 %all-gather.14.cloned.1.call-start = ((), (), s32[]{:S(2)}) async-start(), calls=%async_computation.8 | async-start | bytes 4718592 | tf_op jit(solution)/shard_map/all_gather | solution.py:125
  9.4 157.1 %all-gather.10.cloned.1.call-start = ((), (), s32[]{:S(2)}) async-start(), calls=%async_computation.5 | async-start | bytes 2949120 | tf_op jit(solution)/shard_map/all_gather | solution.py:164
  77.1 22.5 %copy-start.1 = (bf16[1,128,4096]{2,1,0:T(8,128)(2,1)S(1)}, bf16[1,128,4096]{2,1,0:T(8,128)(2,1)}, u32[]{:S(2)}) copy-start(bf16[1,128,4096]{2,1,0:T(8,128)(2,1)} %param.16) | copy-start | bytes 3145732
  77.1 22.5 %copy-start.2 = (bf16[1,128,4096]{2,1,0:T(8,128)(2,1)S(1)}, bf16[1,128,4096]{2,1,0:T(8,128)(2,1)}, u32[]{:S(2)}) copy-start(bf16[1,128,4096]{2,1,0:T(8,128)(2,1)} %param.18) | copy-start | bytes 3145732
  83.9 123.7 %reduce-scatter.2.cloned.1.call-start = ((), (), s32[]{:S(2)}) async-start(), calls=%async_computation.6 | async-start | bytes 2359296 | tf_op jit(solution)/shard_map/reduce_scatter | solution.py:149
  99.5 1.2 copy-start.3
  100.8 1.2 copy-start.4
  173.1 12.4 %copy-start.6 = (f32[1,128,1]{1,2,0:T(1,128)S(1)}, f32[1,128,1]{1,2,0:T(1,128)}, u32[]{:S(2)}) copy-start(f32[1,128,1]{1,2,0:T(1,128)} %param.12) | copy-start | bytes 1540
  173.1 23.2 %all-to-all-start.1 = ((bf16[4,4,48,1024]{3,2,0,1:T(8,128)(2,1)}), bf16[4,4,48,1024]{3,2,0,1:T(8,128)(2,1)S(1)}, u32[]{:S(2)}, u32[]{:S(2)}) async-start(bf16[4,4,48,1024]{3,2,0,1:T(8,128)(2,1)} %copy.16), calls=%async_computation.1 | async-start | bytes 3145728 | tf_op jit(solution)/shard_map/all_to_all | solution.py:169
  196.3 7.8 %all-to-all-start.3 = ((bf16[4,1,48]{2,1,0:T(2,128)(2,1)}), bf16[4,1,48]{2,1,0:T(2,128)(2,1)S(1)}, u32[]{:S(2)}, u32[]{:S(2)}) async-start(bf16[4,1,48]{2,1,0:T(2,128)(2,1)} %convert_element_type.47), calls=%async_computation.3 | async-start | bytes 4096 | tf_op jit(solution)/shard_map/all_to_all | solution.py:187
  204.0 28.0 %all-to-all-start.2 = ((bf16[4,128,1024]{2,1,0:T(8,128)(2,1)}), bf16[4,128,1024]{2,1,0:T(8,128)(2,1)S(1)}, u32[]{:S(2)}, u32[]{:S(2)}) async-start(bf16[4,128,1024]{2,1,0:T(8,128)(2,1)} %multiply_convert_fusion), calls=%async_computation.2 | async-start | bytes 2097152 | tf_op jit(solution)/shard_map/all_to_all | solution.py:183
Sparse Core Ops, SparseCore 0:
  9.6 67.4 all-gather.11
  78.7 20.8 all-gather.15
  101.1 11.7 all-gather.13
  114.8 51.6 all-gather.9
  168.7 34.6 reduce-scatter.1

commit v2 on v1

--- a/solution.py
+++ b/solution.py
@@ -14,7 +14,7 @@
 
 
 def attention_kernel(
-    pairs, pos_ref, q_ref, g_ref, o_ref, kv_ref, dq_ref, dkv_ref, kt_ref, bias_ref, st_ref, ds_ref
+    pairs, pos_ref, q_ref, g_ref, o_ref, kv_ref, dq_ref, out_ref, dkv_ref, kt_ref, bias_ref, st_ref, ds_ref
 ):
     seq_len = kv_ref.shape[0]
     rows = q_ref.shape[0]
@@ -64,6 +64,10 @@
         for i in range(2):
             dq_ref[:, cols[i]] = dq[i * rows : (i + 1) * rows].astype(dq_ref.dtype)
 
+    @pl.when(pl.program_id(1) == pl.num_programs(1) - 1)
+    def _():
+        out_ref[...] = dkv_ref[...].astype(out_ref.dtype)
+
 
 def attention(q, g, o, kv, first):
     rows, width = q.shape
@@ -81,9 +85,10 @@
         out_specs=[tok, key],
         out_shape=[
             jax.ShapeDtypeStruct((rows, width), jnp.bfloat16),
-            jax.ShapeDtypeStruct((seq_len, kv.shape[1]), jnp.float32),
+            jax.ShapeDtypeStruct((seq_len, kv.shape[1]), jnp.bfloat16),
         ],
         scratch_shapes=[
+            pltpu.VMEM((seq_len, 2 * hd), jnp.float32),
             pltpu.VMEM((hd, seq_len), jnp.bfloat16),
             pltpu.VMEM((seq_len, 2 * rows), jnp.float32),
             pltpu.VMEM((pairs, seq_len, 2 * rows), jnp.float32),
@@ -117,14 +122,9 @@
     capacity = saved_pre.shape[2] // experts
     hidden = down_weight.shape[1]
     chips = contexts // 2
-    pair_groups = [[2 * i, 2 * i + 1] for i in range(chips)]
     chip_groups = [[2 * i + core for i in range(chips)] for core in range(2)]
 
-    kv_all = lax.all_gather(keys_values[0], "ctx", axis=0, tiled=True)
-    down_full = lax.all_gather(down_weight[0], "ctx", axis=1, tiled=True)
-    gate_up = lax.all_gather(
-        gate_up_weight[0], "ctx", axis=0, tiled=True, axis_index_groups=pair_groups
-    )
+    swap = [(i, i ^ 1) for i in range(contexts)]
 
     route_rows = routes[0]
     one_hot = (
@@ -134,6 +134,24 @@
     positions = jnp.sum(earlier * one_hot, axis=-1)
     slot_keys = route_rows[:, 0] * capacity + positions
     slots = experts * capacity
+
+    kv_local = keys_values[0]
+    kv_width = kv_local.shape[1]
+    extra = jnp.broadcast_to(
+        jnp.pad(slot_keys.astype(jnp.bfloat16), (0, kv_width - tok_rows))[None], (16, kv_width)
+    )
+    kv_wide = lax.all_gather(jnp.concatenate([kv_local, extra], axis=0), "ctx", axis=0)
+    kv_all = kv_wide[:, :tok_rows].reshape(contexts * tok_rows, kv_width)
+    block_keys = kv_wide[:, tok_rows, :tok_rows].astype(jnp.int32)
+    core = lax.axis_index("ctx") % 2
+    block_keys = block_keys.reshape(chips, 2, tok_rows)
+    block_keys = jnp.where(core == 0, block_keys[:, 0], block_keys[:, 1])
+
+    down_shard, kv_all = lax.optimization_barrier((down_weight[0], kv_all))
+    down_full = lax.all_gather(down_shard, "ctx", axis=1, tiled=True)
+    gate_up_own = gate_up_weight[0]
+    gate_up_other = lax.ppermute(gate_up_own, "ctx", swap)
+
     dispatch = (jnp.arange(slots, dtype=jnp.int32)[:, None] == slot_keys[None, :]).astype(
         jnp.bfloat16
     )
@@ -146,8 +164,12 @@
 
     first = (lax.axis_index("ctx") * tok_rows).astype(jnp.int32).reshape(1)
     query_grad, kv_terms = attention(queries[0], attn_grad[0], attn_out[0], kv_all, first)
-    kv_grad = lax.psum_scatter(kv_terms, "ctx", scatter_dimension=0, tiled=True).astype(
-        jnp.bfloat16
+    kv_back = lax.all_to_all(
+        kv_terms.reshape(contexts, tok_rows, kv_width),
+        "ctx",
+        split_axis=0,
+        concat_axis=0,
+        tiled=True,
     )
 
     down_grad = lax.dot_general(expert_rows, down_full, NT, preferred_element_type=jnp.float32)
@@ -162,8 +184,18 @@
     pre_grad = jnp.concatenate([gate_part, up_part], axis=-1).astype(jnp.bfloat16)
 
     pre_all = lax.all_gather(pre_grad, "ctx", axis=0, tiled=True, axis_index_groups=chip_groups)
-    slot_input = lax.dot_general(pre_all, gate_up, NT, preferred_element_type=jnp.float32).astype(
-        jnp.bfloat16
+    back_prob = lax.all_to_all(
+        slot_prob.reshape(experts, capacity), "exp", split_axis=0, concat_axis=0, tiled=True
+    ).reshape(slots)
+    pre_all, back_prob, kv_back = lax.optimization_barrier((pre_all, back_prob, kv_back))
+    slot_input = jnp.concatenate(
+        [
+            lax.dot_general(pre_all, part, NT, preferred_element_type=jnp.float32).astype(
+                jnp.bfloat16
+            )
+            for part in (gate_up_own, gate_up_other)
+        ],
+        axis=1,
     )
     columns = slot_input.shape[1]
     back = lax.all_to_all(
@@ -173,21 +205,22 @@
         concat_axis=1,
         tiled=True,
     ).reshape(chips, slots, columns)
-    keys_all, gates_all = (
-        lax.all_gather(item, "ctx", axis=0, axis_index_groups=chip_groups)
-        for item in (slot_keys, gate_probs[0, :, 0])
-    )
-    pick = (keys_all[:, :, None] == jnp.arange(slots, dtype=jnp.int32)).astype(jnp.bfloat16)
-    picked = jnp.einsum("cts,csd->ctd", pick, back, preferred_element_type=jnp.float32)
-    combined = (gates_all[:, :, None] * picked).astype(jnp.bfloat16)
+    pick = (block_keys[:, :, None] == jnp.arange(slots, dtype=jnp.int32)).astype(jnp.bfloat16)
+    picked = jnp.einsum("cts,csd->ctd", pick, back, preferred_element_type=jnp.float32).astype(
+        jnp.bfloat16
+    )
     returned = lax.all_to_all(
-        combined, "ctx", split_axis=0, concat_axis=0, tiled=True, axis_index_groups=chip_groups
-    )
-    moe_input_grad = returned.transpose(1, 0, 2).reshape(1, tok_rows, width)
-    back_prob = lax.all_to_all(
-        slot_prob.reshape(experts, capacity), "exp", split_axis=0, concat_axis=0, tiled=True
-    ).reshape(slots)
-    prob_grad = back_prob[slot_keys][None, :, None]
+        picked, "ctx", split_axis=0, concat_axis=0, tiled=True, axis_index_groups=chip_groups
+    )
+    gated = gate_probs[0][None] * returned.astype(jnp.float32)
+    gated = gated.astype(jnp.bfloat16).transpose(1, 0, 2).reshape(tok_rows, chips, 2, columns // 2)
+    gated = jnp.where(core == 0, gated, gated[:, :, ::-1])
+    moe_input_grad = gated.reshape(1, tok_rows, width)
+    own_slots = slot_keys[:, None] == jnp.arange(slots, dtype=jnp.int32)
+    prob_grad = jnp.sum(
+        jnp.where(own_slots, back_prob.astype(jnp.float32), 0.0), axis=1
+    ).astype(jnp.bfloat16)[None, :, None]
+    kv_grad = jnp.sum(kv_back.astype(jnp.float32), axis=0).astype(jnp.bfloat16)
     return (moe_input_grad, prob_grad, query_grad[None], kv_grad[None])
 
 

time: 241 us -> 262 us (1.087)
  waiting for transfers between devices: 125 us -> 144 us
  blocking collectives: 42 us -> 23.8 us
  local copies, waits for them, and re-layouts: 8.48 us -> 17.9 us
  other arithmetic: 2.95 us -> 7.71 us
  starting transfers between devices: 10.7 us -> 15.2 us
    all_gather x1, waiting for transfers between devices: 40.2 us -> 0.01 us  [body(): lax.all_gather(pre_grad, 'ctx', axis=0, tiled=True, axis_index_groups=chi...]
    all_to_all x1 -> x2, waiting for transfers between devices: 21 us -> 59.5 us  [the longest x1 36 us: body(): lax.all_to_all(kv_terms.reshape(contexts, tok_rows, kv_width), 'ctx', spl...]
    all_to_all x1, waiting for transfers between devices: 1.51 us -> 18.7 us  [body(): lax.all_to_all(slot_input.reshape(chips, experts, capacity, columns), 'ex...]
    all_gather x2 -> x0, blocking collectives: 17.2 us -> none  [body(): lax.all_gather(item, 'ctx', axis=0, axis_index_groups=chip_groups)]
    all_gather x3 -> x2, waiting for transfers between devices: 57.3 us -> 65.7 us  [the longest x1 40.3 us: body(): down_full = lax.all_gather(down_shard, 'ctx', axis=1, tiled=True)]
    rev x0 -> x1, local copies, waits for them, and re-layouts: none -> 5.52 us  [body(): gated = jnp.where(core == 0, gated, gated[:, :, ::-1])]
    all_to_all x1 -> x2, starting transfers between devices: 3.52 us -> 7.39 us  [the longest x1 3.83 us: body(): lax.all_to_all(picked, 'ctx', split_axis=0, concat_axis=0, tiled=True, ax...]
    all_to_all x1, waiting for transfers between devices: 2.85 us -> 0.01 us  [body(): lax.all_to_all(slot_prob.reshape(experts, capacity), 'exp', split_axis=0,...]
  transfers between devices with their start and end apart: 8 -> 8, of which waited for: 6 -> 5; matrix products, arithmetic and copies ran while one was open for 8% -> 3% of each run, Pallas kernels for 10% -> 9%
where the time goes in v2:
time: 262 us
  waiting for transfers between devices  144 us (55%)
  Pallas kernels  24.4 us (9%)
  blocking collectives  23.8 us (9%)
  local copies, waits for them, and re-layouts  17.9 us (7%)
  starting transfers between devices  15.2 us (6%)
  matrix products  14.6 us (6%)
  between operations  14 us (5%)
  other arithmetic  7.71 us (3%)
    all_gather x1, waiting for transfers between devices, body(): down_full = lax.all_gather(down_shard, 'ctx', axis=1, tiled=True)  40.3 us
    all_to_all x1, waiting for transfers between devices, body(): lax.all_to_all(kv_terms.reshape(contexts, tok_rows, kv_width), 'ctx', spl...  36 us
    all_gather x1, waiting for transfers between devices, body(): lax.all_gather(jnp.concatenate([kv_local, extra], axis=0), 'ctx', axis=0)  25.5 us
    pallas_call x1, Pallas kernels, attention(): pl.pallas_call(functools.partial(attention_kernel, pairs), grid=(KEY_VALU...  24.4 us
    all_to_all x1, blocking collectives, body(): lax.all_to_all(send_rows.reshape(experts, capacity, width), 'exp', split_...  23.8 us
    all_to_all x1, waiting for transfers between devices, body(): lax.all_to_all(picked, 'ctx', split_axis=0, concat_axis=0, tiled=True, ax...  23.5 us
    all_to_all x1, waiting for transfers between devices, body(): lax.all_to_all(slot_input.reshape(chips, experts, capacity, columns), 'ex...  18.7 us
    dot_general x2, matrix products, body(): lax.dot_general(pre_all, part, NT, preferred_element_type=jnp.float32)  6.8 us
  transfers between devices with their start and end apart: 8, of which 5 were waited for; matrix products, arithmetic and copies ran while one was open for 3% of the time, Pallas kernels for 9%

profile of v2, /device:TPU:0, one launch (start us, length us, event | category | flops | bytes accessed | tf_op | source)
XLA Modules:
  0.0 261.6 jit_solution(18075369445044102393)
XLA Ops:
  7.2 0.0 copy-start
  7.2 0.0 all-gather.9.cloned.1.call-start
  7.2 0.8 fusion.12
  8.0 0.2 reduce_window_sum.11
  8.2 0.8 select_reduce_fusion.1
  9.1 0.7 fusion.16
  9.7 1.6 pad_maximum_fusion.2
  11.3 0.0 all-gather.9.cloned.1.call-update
  11.3 0.0 all-gather.5.cloned.1.call-start
  11.4 25.5 %all-gather.9.cloned.1.call-done = bf16[1152,512]{1,0:T(8,128)(2,1)} async-done(((bf16[144,512]{1,0:T(8,128)(2,1)}), bf16[1152,512]{1,0:T(8,128)(2,1)}) %all-gather.9.cloned.1.call-update) | async-done | bytes 1179664 | tf_op jit(solution)/shard_map/all_gather | solution.py:143
  36.8 1.3 slice.27
  38.2 0.0 all-gather.5.cloned.1.call-update
  38.2 0.0 all-gather.7.cloned.1.call-start
  38.3 0.6 convolution_convert_fusion
  38.8 23.8 %all_to_all.26 = bf16[4,48,4096]{2,1,0:T(8,128)(2,1)} all-to-all(bf16[4,48,4096]{2,1,0:T(8,128)(2,1)S(1)} %bitcast.54), channel_id=1, replica_groups=mesh['ctx'=8,'exp'=4] {'exp'}, dimensions={0} | all-to-all | bytes 3145728 | tf_op jit(solution)/shard_map/all_to_all | solution.py:161
  62.7 40.3 %all-gather.5.cloned.1.call-done = bf16[768,4096]{1,0:T(8,128)(2,1)} async-done(((bf16[768,512]{1,0:T(8,128)(2,1)}), bf16[768,4096]{1,0:T(8,128)(2,1)}) %all-gather.5.cloned.1.call-update) | async-done | bytes 6291472 | tf_op jit(solution)/shard_map/all_gather | solution.py:151
  103.0 5.8 %fusion.5 = (bf16[192]{0:T(256)(128)(2,1)S(1)}, bf16[192,768]{1,0:T(8,128)(2,1)S(1)}, bf16[192,768]{1,0:T(8,128)(2,1)S(1)}) fusion(bf16[192,1536]{1,0:T(8,128)(2,1)S(1)} %bitcast.71, bf16[192,4096]{1,0:T(8,128)(2,1)} %bitcast.57, bf16[768,4096]{1,0:T(8,128)(2,1)} %all-gather.5.cloned.1.call-done), kind=kOutput, calls=%fused_computation.17 | convolution fusion | flops 1210466048 | bytes 9044352 | tf_op jit(solution)/shard_map/dot_general | solution.py:175
  108.8 0.9 pad_maximum_fusion.1
  109.6 0.0 all-gather.7.cloned.1.call-update
  109.7 0.7 convert_element_type.92
  110.3 3.6 %all-to-all-start.1 = ((bf16[4,1,48]{2,1,0:T(2,128)(2,1)}), bf16[4,1,48]{2,1,0:T(2,128)(2,1)S(1)}, u32[]{:S(2)}, u32[]{:S(2)}) async-start(bf16[4,1,48]{2,1,0:T(2,128)(2,1)} %convert_element_type.92), calls=%async_computation.1 | async-start | bytes 4096 | tf_op jit(solution)/shard_map/all_to_all | solution.py:187
  114.0 1.3 copy-done.2
  115.3 1.3 copy-done.3
  116.6 24.4 %shard_map.129 = (bf16[128,4096]{1,0:T(8,128)(2,1)}, bf16[1024,512]{1,0:T(8,128)(2,1)}) custom-call(s32[1]{0:T(128)} %bitcast.12.pos_ref, bf16[128,4096]{1,0:T(8,128)(2,1)S(1)} %bitcast.48, bf16[128,4096]{1,0:T(8,128)(2,1)S(1)} %bitcast.49, bf16[128,4096]{1,0:T(8,128)(2,1)S(1)} %bitcast.50, bf16[1024,512]{1,0:T(8,128)(2,1)S(1)} %bitcast.47), custom_call_target="tpu_custom_call" | custom-call | flops 5368709120 | bytes 7340032 | tf_op jit(solution)/shard_map/pallas_call | solution.py:81
  140.9 3.6 %all-to-all-start.2 = ((bf16[8,128,512]{2,1,0:T(8,128)(2,1)}), bf16[8,128,512]{2,1,0:T(8,128)(2,1)S(1)}, u32[]{:S(2)}, u32[]{:S(2)}) async-start(bf16[8,128,512]{2,1,0:T(8,128)(2,1)} %bitcast.16), calls=%async_computation.2 | async-start | bytes 2097152 | tf_op jit(solution)/shard_map/all_to_all | solution.py:167
  144.5 0.4 collective-permute-start
  144.9 0.1 reshape.98
  145.0 36.0 %all-to-all-done.2 = bf16[8,128,512]{2,1,0:T(8,128)(2,1)S(1)} async-done(((bf16[8,128,512]{2,1,0:T(8,128)(2,1)}), bf16[8,128,512]{2,1,0:T(8,128)(2,1)S(1)}, u32[]{:S(2)}, u32[]{:S(2)}) %all-to-all-start.2) | async-done | bytes 1048608 | tf_op jit(solution)/shard_map/all_to_all | solution.py:167
  181.0 4.0 %convolution_convert_fusion.3 = bf16[768,512]{0,1:T(8,128)(2,1)S(1)} fusion(bf16[768,1536]{1,0:T(8,128)(2,1)} %all-gather.7.cloned.1.call-done, bf16[1,512,1536]{2,1,0:T(8,128)(2,1)} %param.15), kind=kOutput, calls=%fused_computation.6 | convolution fusion | flops 1208352768 | bytes 4718592 | tf_op jit(solution)/shard_map/dot_general | solution.py:193
  185.0 2.8 %convolution_convert_fusion.2 = bf16[768,512]{0,1:T(8,128)(2,1)S(1)} fusion(bf16[768,1536]{1,0:T(8,128)(2,1)S(1)} %copy-done.7, bf16[512,1536]{1,0:T(8,128)(2,1)} %collective-permute-done), kind=kOutput, calls=%fused_computation.5 | convolution fusion | flops 1208352768 | bytes 4718592 | tf_op jit(solution)/shard_map/dot_general | solution.py:193
  187.8 0.1 pad_maximum_fusion
  187.9 1.6 copy.32
  189.6 2.7 %copy.33 = bf16[4,4,48,1024]{3,2,0,1:T(8,128)(2,1)} copy(bf16[4,4,48,1024]{3,2,1,0:T(8,128)(2,1)} %bitcast.53) | data formatting | bytes 3145728 | tf_op jit(solution)/shard_map/reshape | solution.py:202
  192.3 3.7 %all-to-all-start.3 = ((bf16[4,4,48,1024]{3,2,0,1:T(8,128)(2,1)}), bf16[4,4,48,1024]{3,2,0,1:T(8,128)(2,1)S(1)}, u32[]{:S(2)}, u32[]{:S(2)}) async-start(bf16[4,4,48,1024]{3,2,0,1:T(8,128)(2,1)} %copy.33), calls=%async_computation.3 | async-start | bytes 3145728 | tf_op jit(solution)/shard_map/all_to_all | solution.py:201
  196.0 0.7 slice_convert_fusion
  196.7 18.7 %all-to-all-done.3 = bf16[4,4,48,1024]{3,2,0,1:T(8,128)(2,1)S(1)} async-done(((bf16[4,4,48,1024]{3,2,0,1:T(8,128)(2,1)}), bf16[4,4,48,1024]{3,2,0,1:T(8,128)(2,1)S(1)}, u32[]{:S(2)}, u32[]{:S(2)}) %all-to-all-start.3) | async-done | bytes 1572896 | tf_op jit(solution)/shard_map/all_to_all | solution.py:201
  215.5 0.1 copy.34
  215.6 1.5 convolution_convert_fusion.1
  217.1 3.8 %all-to-all-start.4 = ((bf16[4,128,1024]{2,1,0:T(8,128)(2,1)}), bf16[4,128,1024]{2,1,0:T(8,128)(2,1)S(1)}, u32[]{:S(2)}, u32[]{:S(2)}) async-start(bf16[4,128,1024]{2,1,0:T(8,128)(2,1)} %convolution_convert_fusion.1), calls=%async_computation.4 | async-start | bytes 2097152 | tf_op jit(solution)/shard_map/all_to_all | solution.py:212
  220.9 0.8 reduce_sum.42
  221.8 0.6 select_reduce_fusion
  222.4 23.5 %all-to-all-done.4 = bf16[4,128,1024]{2,1,0:T(8,128)(2,1)S(1)} async-done(((bf16[4,128,1024]{2,1,0:T(8,128)(2,1)}), bf16[4,128,1024]{2,1,0:T(8,128)(2,1)S(1)}, u32[]{:S(2)}, u32[]{:S(2)}) %all-to-all-start.4) | async-done | bytes 1048608 | tf_op jit(solution)/shard_map/all_to_all | solution.py:212
  245.9 0.4 fusion
  246.3 0.8 reshape.103
  247.1 5.5 %rev.3 = bf16[128,4,2,512]{3,2,0,1:T(2,128)(2,1)S(1)} reverse(bf16[128,4,2,512]{3,2,0,1:T(2,128)(2,1)S(1)} %reshape.103), dimensions={2} | reverse | bytes 2097152 | tf_op jit(solution)/shard_map/rev | solution.py:217
  252.6 0.1 broadcast_select_fusion
  252.8 0.7 copy.35
  253.5 1.6 reshape.104
  (24 shorter events, 0.1 us)
Async XLA Ops:
  7.2 31.1 %copy-start = (bf16[1,128,4096]{2,1,0:T(8,128)(2,1)S(1)}, bf16[1,128,4096]{2,1,0:T(8,128)(2,1)}, u32[]{:S(2)}) copy-start(bf16[1,128,4096]{2,1,0:T(8,128)(2,1)} %param.10) | copy-start | bytes 3145732
  7.2 29.7 %all-gather.9.cloned.1.call-start = ((), (), s32[]{:S(2)}) async-start(), calls=%async_computation.7 | async-start | bytes 1327104 | tf_op jit(solution)/shard_map/all_gather | solution.py:143
  11.3 91.6 %all-gather.5.cloned.1.call-start = ((), (), s32[]{:S(2)}) async-start(), calls=%async_computation.5 | async-start | bytes 7077888 | tf_op jit(solution)/shard_map/all_gather | solution.py:151
  38.2 142.8 %all-gather.7.cloned.1.call-start = ((), (), s32[]{:S(2)}) async-start(), calls=%async_computation.6 | async-start | bytes 2949120 | tf_op jit(solution)/shard_map/all_gather | solution.py:186
  38.8 64.1 %copy-start.8 = (bf16[1,1,192,1536]{3,2,1,0:T(8,128)(2,1)S(1)}, bf16[1,1,192,1536]{3,2,1,0:T(8,128)(2,1)}, u32[]{:S(2)}) copy-start(bf16[1,1,192,1536]{3,2,1,0:T(8,128)(2,1)} %param.13) | copy-start | bytes 1769476
  108.7 5.2 %copy-start.1 = (bf16[1,128,4096]{2,1,0:T(8,128)(2,1)S(1)}, bf16[1,128,4096]{2,1,0:T(8,128)(2,1)}, u32[]{:S(2)}) copy-start(bf16[1,128,4096]{2,1,0:T(8,128)(2,1)} %param.16) | copy-start | bytes 3145732
  110.3 30.6 %all-to-all-start.1 = ((bf16[4,1,48]{2,1,0:T(2,128)(2,1)}), bf16[4,1,48]{2,1,0:T(2,128)(2,1)S(1)}, u32[]{:S(2)}, u32[]{:S(2)}) async-start(bf16[4,1,48]{2,1,0:T(2,128)(2,1)} %convert_element_type.92), calls=%async_computation.1 | async-start | bytes 4096 | tf_op jit(solution)/shard_map/all_to_all | solution.py:187
  114.0 1.3 copy-start.2
  115.3 1.3 copy-start.3
  140.9 40.1 %all-to-all-start.2 = ((bf16[8,128,512]{2,1,0:T(8,128)(2,1)}), bf16[8,128,512]{2,1,0:T(8,128)(2,1)S(1)}, u32[]{:S(2)}, u32[]{:S(2)}) async-start(bf16[8,128,512]{2,1,0:T(8,128)(2,1)} %bitcast.16), calls=%async_computation.2 | async-start | bytes 2097152 | tf_op jit(solution)/shard_map/all_to_all | solution.py:167
  144.5 40.5 %collective-permute-start = (bf16[512,1536]{1,0:T(8,128)(2,1)}, bf16[512,1536]{1,0:T(8,128)(2,1)}, u32[]{:S(2)}, u32[]{:S(2)}) collective-permute-start(bf16[512,1536]{1,0:T(8,128)(2,1)} %bitcast.70), channel_id=1, source_target_pairs={{0,4},{4,0},{8,12},{12,8},{16,20},{20,16},{24,28},{28,24},{1,5},{5... | collective-permute-start | bytes 4718600 | tf_op jit(solution)/shard_map/ppermute | solution.py:153
  181.0 4.0 %copy-start.4 = (bf16[8,128,512]{2,1,0:T(8,128)(2,1)}, bf16[8,128,512]{2,1,0:T(8,128)(2,1)S(1)}, u32[]{:S(2)}) copy-start(bf16[8,128,512]{2,1,0:T(8,128)(2,1)S(1)} %all-to-all-done.2) | copy-start | bytes 3145732
  181.0 4.0 %copy-start.7 = (bf16[768,1536]{1,0:T(8,128)(2,1)S(1)}, bf16[768,1536]{1,0:T(8,128)(2,1)}, u32[]{:S(2)}) copy-start(bf16[768,1536]{1,0:T(8,128)(2,1)} %all-gather.7.cloned.1.call-done) | copy-start | bytes 7077892
  192.3 23.2 %all-to-all-start.3 = ((bf16[4,4,48,1024]{3,2,0,1:T(8,128)(2,1)}), bf16[4,4,48,1024]{3,2,0,1:T(8,128)(2,1)S(1)}, u32[]{:S(2)}, u32[]{:S(2)}) async-start(bf16[4,4,48,1024]{3,2,0,1:T(8,128)(2,1)} %copy.33), calls=%async_computation.3 | async-start | bytes 3145728 | tf_op jit(solution)/shard_map/all_to_all | solution.py:201
  217.1 3.9 %copy-start.5 = (bf16[8,128,512]{2,1,0:T(8,128)(2,1)S(1)}, bf16[8,128,512]{2,1,0:T(8,128)(2,1)}, u32[]{:S(2)}) copy-start(bf16[8,128,512]{2,1,0:T(8,128)(2,1)} %copy-done.4) | copy-start | bytes 3145732
  217.1 28.8 %copy-start.6 = (f32[1,128,1]{1,2,0:T(1,128)S(1)}, f32[1,128,1]{1,2,0:T(1,128)}, u32[]{:S(2)}) copy-start(f32[1,128,1]{1,2,0:T(1,128)} %param.12) | copy-start | bytes 1540
  217.1 28.8 %all-to-all-start.4 = ((bf16[4,128,1024]{2,1,0:T(8,128)(2,1)}), bf16[4,128,1024]{2,1,0:T(8,128)(2,1)S(1)}, u32[]{:S(2)}, u32[]{:S(2)}) async-start(bf16[4,128,1024]{2,1,0:T(8,128)(2,1)} %convolution_convert_fusion.1), calls=%async_computation.4 | async-start | bytes 2097152 | tf_op jit(solution)/shard_map/all_to_all | solution.py:212
Sparse Core Ops, SparseCore 0:
  11.5 25.3 all-gather.8
  38.4 64.4 all-gather.4
  109.8 59.0 all-gather.6

commit v3 on v2

--- a/solution.py
+++ b/solution.py
@@ -103,6 +103,243 @@
     )(first, q, g, o, kv)
 
 
+MESH = pl.DeviceIdType.MESH
+
+
+def return_kernel(
+    chips,
+    experts,
+    pre_ref,
+    gu_ref,
+    pick_ref,
+    gate_ref,
+    out_ref,
+    pre_buf,
+    gu_buf,
+    sent,
+    came,
+    leaving,
+    landed,
+    pair_sems,
+    up_sems,
+    down_sems,
+    pre_sems,
+    cross_out,
+    cross_in,
+    back_out,
+    back_in,
+):
+    me = lax.axis_index("ctx")
+    mine = lax.axis_index("exp")
+    z = lax.div(me, 2)
+    core = lax.rem(me, 2)
+    shard = gu_ref.shape[0]
+    columns = 2 * shard
+    tile = min(shard, 256)
+
+    barrier = pltpu.get_barrier_semaphore()
+    for d in range(1, chips):
+        chip = lax.rem(z + d, chips)
+        pl.semaphore_signal(
+            barrier, inc=1, device_id={"ctx": 2 * chip + core}, device_id_type=MESH
+        )
+    for d in range(1, experts):
+        pl.semaphore_signal(
+            barrier, inc=1, device_id={"exp": lax.rem(mine + d, experts)}, device_id_type=MESH
+        )
+    other = 2 * z + 1 - core
+    pl.semaphore_signal(barrier, inc=1, device_id={"ctx": other}, device_id_type=MESH)
+    pre_buf[z] = pre_ref[...]
+    pl.semaphore_wait(barrier, chips + experts - 1)
+
+    def remote(src, dst, send, recv, device):
+        return pltpu.make_async_remote_copy(
+            src_ref=src,
+            dst_ref=dst,
+            send_sem=send,
+            recv_sem=recv,
+            device_id=device,
+            device_id_type=MESH,
+        )
+
+    def up(b):
+        return remote(
+            pre_buf.at[b], pre_buf.at[b], up_sems.at[b], pre_sems.at[b], {"ctx": me + 2}
+        )
+
+    def down(b):
+        return remote(
+            pre_buf.at[b], pre_buf.at[b], down_sems.at[b], pre_sems.at[b], {"ctx": me - 2}
+        )
+
+    def cross(b, to, slot):
+        return remote(
+            sent.at[b, to], came.at[b, slot], cross_out.at[b, to], cross_in.at[b, slot], {"exp": to}
+        )
+
+    def back(b, slot):
+        return remote(
+            leaving.at[b],
+            landed.at[slot],
+            back_out.at[b],
+            back_in.at[slot],
+            {"ctx": 2 * b + core},
+        )
+
+    swap = remote(
+        gu_ref, gu_buf.at[core], pair_sems.at[0], pair_sems.at[1], {"ctx": other}
+    )
+    has_up = z + 1 < chips
+    has_down = z > 0
+
+    @pl.when(has_up)
+    def _():
+        up(z).start()
+
+    @pl.when(has_down)
+    def _():
+        down(z).start()
+
+    swap.start()
+    gu_buf[core] = gu_ref[...]
+    swap.wait_recv()
+
+    def block_of(i):
+        ahead = lax.rem(z + i, chips)
+        behind = lax.rem(z - i + chips, chips)
+        return jnp.where(z < chips // 2, ahead, behind)
+
+    def combine(b):
+        for d in range(1, experts):
+            j = lax.rem(mine + d, experts)
+            cross(b, j, j).wait_recv()
+        slots = pick_ref.shape[2]
+        for t in range(columns // tile):
+            cols = pl.ds(t * tile, tile)
+            rows = came[b, :, :, cols].reshape(slots, tile)
+            leaving[b, :, cols] = jnp.dot(
+                pick_ref[b], rows, preferred_element_type=jnp.float32
+            ).astype(leaving.dtype)
+
+        @pl.when(b != z)
+        def _():
+            back(b, z).start()
+
+        @pl.when(b == z)
+        def _():
+            landed[z] = leaving[b]
+
+    def turn(i, carry):
+        lo = z - i
+        hi = z + i
+
+        @pl.when((i > 0) & (lo >= 0))
+        def _():
+            up(lo).wait_recv()
+
+            @pl.when(has_up)
+            def _():
+                up(lo).start()
+
+        @pl.when((i > 0) & (hi < chips))
+        def _():
+            down(hi).wait_recv()
+
+            @pl.when(has_down)
+            def _():
+                down(hi).start()
+
+        b = block_of(i)
+        for half in range(2):
+            for t in range(shard // tile):
+                weights = gu_buf[half, pl.ds(t * tile, tile), :]
+                grads = lax.dot_general(
+                    pre_buf[b], weights, NT, preferred_element_type=jnp.float32
+                )
+                cols = pl.ds(half * shard + t * tile, tile)
+                sent[b, :, :, cols] = grads.astype(sent.dtype).reshape(experts, -1, tile)
+        for d in range(1, experts):
+            cross(b, lax.rem(mine + d, experts), mine).start()
+        came[b, mine] = sent[b, mine]
+
+        @pl.when(i > 0)
+        def _():
+            combine(block_of(i - 1))
+
+        return carry
+
+    lax.fori_loop(0, chips, turn, 0)
+    combine(block_of(chips - 1))
+    for b in range(chips):
+
+        @pl.when(z != b)
+        def _():
+            back(b, b).wait_recv()
+
+        out_ref[:, pl.ds(b * columns, columns)] = (
+            gate_ref[...] * landed[b].astype(jnp.float32)
+        ).astype(out_ref.dtype)
+
+    swap.wait_send()
+    for b in range(chips):
+
+        @pl.when(has_up & (z >= b))
+        def _():
+            up(b).wait_send()
+
+        @pl.when(has_down & (z <= b))
+        def _():
+            down(b).wait_send()
+
+        @pl.when(z != b)
+        def _():
+            back(b, z).wait_send()
+
+        for d in range(1, experts):
+            cross(b, lax.rem(mine + d, experts), mine).wait_send()
+
+
+def expert_return(pre_grad, gate_up, pick, gates, chips, experts):
+    slots, pre_width = pre_grad.shape
+    capacity = slots // experts
+    shard = gate_up.shape[0]
+    tok_rows = gates.shape[0]
+    columns = 2 * shard
+    vmem = pl.BlockSpec(memory_space=pltpu.VMEM)
+    low = jnp.bfloat16
+    dma = pltpu.SemaphoreType.DMA
+    return pl.pallas_call(
+        functools.partial(return_kernel, chips, experts),
+        in_specs=[vmem] * 4,
+        out_specs=vmem,
+        out_shape=jax.ShapeDtypeStruct((tok_rows, chips * columns), low),
+        scratch_shapes=[
+            pltpu.VMEM((chips, slots, pre_width), low),
+            pltpu.VMEM((2, shard, pre_width), low),
+            pltpu.VMEM((chips, experts, capacity, columns), low),
+            pltpu.VMEM((chips, experts, capacity, columns), low),
+            pltpu.VMEM((chips, tok_rows, columns), low),
+            pltpu.VMEM((chips, tok_rows, columns), low),
+            dma((2,)),
+            dma((chips,)),
+            dma((chips,)),
+            dma((chips,)),
+            dma((chips, experts)),
+            dma((chips, experts)),
+            dma((chips,)),
+            dma((chips,)),
+        ],
+        compiler_params=pltpu.CompilerParams(
+            collective_id=0, has_side_effects=True, vmem_limit_bytes=40 * 1024 * 1024
+        ),
+        cost_estimate=pl.CostEstimate(
+            flops=2 * chips * slots * pre_width * columns,
+            bytes_accessed=4 * (slots * pre_width + shard * pre_width),
+            transcendentals=0,
+        ),
+    )(pre_grad, gate_up, pick, gates)
+
+
 def body(
     grad_out,
     routes,
@@ -119,12 +356,10 @@
     contexts = lax.axis_size("ctx")
     tok_rows = grad_out.shape[1]
     width = grad_out.shape[2]
-    capacity = saved_pre.shape[2] // experts
+    filled = saved_pre.shape[2] // experts
+    capacity = -(-filled // 16) * 16
     hidden = down_weight.shape[1]
     chips = contexts // 2
-    chip_groups = [[2 * i + core for i in range(chips)] for core in range(2)]
-
-    swap = [(i, i ^ 1) for i in range(contexts)]
 
     route_rows = routes[0]
     one_hot = (
@@ -149,8 +384,6 @@
 
     down_shard, kv_all = lax.optimization_barrier((down_weight[0], kv_all))
     down_full = lax.all_gather(down_shard, "ctx", axis=1, tiled=True)
-    gate_up_own = gate_up_weight[0]
-    gate_up_other = lax.ppermute(gate_up_own, "ctx", swap)
 
     dispatch = (jnp.arange(slots, dtype=jnp.int32)[:, None] == slot_keys[None, :]).astype(
         jnp.bfloat16
@@ -174,6 +407,10 @@
 
     down_grad = lax.dot_general(expert_rows, down_full, NT, preferred_element_type=jnp.float32)
     pre_acts = saved_pre[0, 0]
+    if capacity != filled:
+        pre_acts = pre_acts.reshape(experts, filled, 2 * hidden)
+        pre_acts = jnp.pad(pre_acts, ((0, 0), (0, capacity - filled), (0, 0)))
+        pre_acts = pre_acts.reshape(slots, 2 * hidden)
     gate_pre = pre_acts[:, :hidden].astype(jnp.float32)
     up_pre = pre_acts[:, hidden:].astype(jnp.float32)
     sigma = jax.nn.sigmoid(gate_pre)
@@ -183,39 +420,14 @@
     up_part = down_grad * swish
     pre_grad = jnp.concatenate([gate_part, up_part], axis=-1).astype(jnp.bfloat16)
 
-    pre_all = lax.all_gather(pre_grad, "ctx", axis=0, tiled=True, axis_index_groups=chip_groups)
     back_prob = lax.all_to_all(
         slot_prob.reshape(experts, capacity), "exp", split_axis=0, concat_axis=0, tiled=True
     ).reshape(slots)
-    pre_all, back_prob, kv_back = lax.optimization_barrier((pre_all, back_prob, kv_back))
-    slot_input = jnp.concatenate(
-        [
-            lax.dot_general(pre_all, part, NT, preferred_element_type=jnp.float32).astype(
-                jnp.bfloat16
-            )
-            for part in (gate_up_own, gate_up_other)
-        ],
-        axis=1,
-    )
-    columns = slot_input.shape[1]
-    back = lax.all_to_all(
-        slot_input.reshape(chips, experts, capacity, columns),
-        "exp",
-        split_axis=1,
-        concat_axis=1,
-        tiled=True,
-    ).reshape(chips, slots, columns)
+    pre_grad, back_prob, kv_back = lax.optimization_barrier((pre_grad, back_prob, kv_back))
     pick = (block_keys[:, :, None] == jnp.arange(slots, dtype=jnp.int32)).astype(jnp.bfloat16)
-    picked = jnp.einsum("cts,csd->ctd", pick, back, preferred_element_type=jnp.float32).astype(
-        jnp.bfloat16
-    )
-    returned = lax.all_to_all(
-        picked, "ctx", split_axis=0, concat_axis=0, tiled=True, axis_index_groups=chip_groups
-    )
-    gated = gate_probs[0][None] * returned.astype(jnp.float32)
-    gated = gated.astype(jnp.bfloat16).transpose(1, 0, 2).reshape(tok_rows, chips, 2, columns // 2)
-    gated = jnp.where(core == 0, gated, gated[:, :, ::-1])
-    moe_input_grad = gated.reshape(1, tok_rows, width)
+    moe_input_grad = expert_return(
+        pre_grad, gate_up_weight[0], pick, gate_probs[0], chips, experts
+    )[None]
     own_slots = slot_keys[:, None] == jnp.arange(slots, dtype=jnp.int32)
     prob_grad = jnp.sum(
         jnp.where(own_slots, back_prob.astype(jnp.float32), 0.0), axis=1

time: 262 us -> 248 us (0.947)
  Pallas kernels: 24.4 us -> 88.3 us
  waiting for transfers between devices: 144 us -> 108 us
  blocking collectives: 23.8 us -> 0 us
  local copies, waits for them, and re-layouts: 17.9 us -> 8.02 us
  matrix products: 14.6 us -> 8.3 us
  starting transfers between devices: 15.2 us -> 11.8 us
    pallas_call x0 -> x1, Pallas kernels: none -> 63.9 us  [expert_return(): pl.pallas_call(functools.partial(return_kernel, chips, experts), in_specs...]
    all_to_all x1 -> x0, blocking collectives: 23.8 us -> none  [body(): lax.all_to_all(send_rows.reshape(experts, capacity, width), 'exp', split_...]
    all_to_all x2 -> x1, waiting for transfers between devices: 42.3 us -> 20 us  [body(): lax.all_to_all(send_rows.reshape(experts, capacity, width), 'exp', split_...]
    all_to_all x1, waiting for transfers between devices: 36 us -> 24.4 us  [body(): lax.all_to_all(kv_terms.reshape(contexts, tok_rows, kv_width), 'ctx', spl...]
    dot_general x3 -> x0, matrix products: 8.26 us -> none  [the longest x2 6.8 us: body(): lax.dot_general(pre_all, part, NT, preferred_element_type=jnp.float32)]
    rev x1 -> x0, local copies, waits for them, and re-layouts: 5.52 us -> none  [body(): gated = jnp.where(core == 0, gated, gated[:, :, ::-1])]
    reshape x3 -> x0, local copies, waits for them, and re-layouts: 5.14 us -> none  [the longest x1 2.73 us: body(): slot_input.reshape(chips, experts, capacity, columns)]
    unnamed x18 -> x15, local copies, waits for them, and re-layouts: 2.64 us -> 5.81 us
  transfers between devices with their start and end apart: 8 -> 5, of which waited for: 5 -> 4; matrix products, arithmetic and copies ran while one was open for 3% -> 2% of each run, Pallas kernels for 9% -> 10%
where the time goes in v3:
time: 248 us
  waiting for transfers between devices  108 us (44%)
  Pallas kernels  88.3 us (36%)
  between operations  14.2 us (6%)
  starting transfers between devices  11.8 us (5%)
  other arithmetic  8.63 us (3%)
  matrix products  8.3 us (3%)
  local copies, waits for them, and re-layouts  8.02 us (3%)
    pallas_call x1, Pallas kernels, expert_return(): pl.pallas_call(functools.partial(return_kernel, chips, experts), in_specs...  63.9 us
    all_gather x1, waiting for transfers between devices, body(): down_full = lax.all_gather(down_shard, 'ctx', axis=1, tiled=True)  38.6 us
    all_gather x1, waiting for transfers between devices, body(): lax.all_gather(jnp.concatenate([kv_local, extra], axis=0), 'ctx', axis=0)  25.5 us
    all_to_all x1, waiting for transfers between devices, body(): lax.all_to_all(kv_terms.reshape(contexts, tok_rows, kv_width), 'ctx', spl...  24.4 us
    pallas_call x1, Pallas kernels, attention(): pl.pallas_call(functools.partial(attention_kernel, pairs), grid=(KEY_VALU...  24.3 us
    all_to_all x1, waiting for transfers between devices, body(): lax.all_to_all(send_rows.reshape(experts, capacity, width), 'exp', split_...  20 us
    dot_general x1, matrix products, body(): lax.dot_general(expert_rows, down_full, NT, preferred_element_type=jnp.fl...  6.51 us
    unnamed x15, local copies, waits for them, and re-layouts  5.81 us
  transfers between devices with their start and end apart: 5, of which 4 were waited for; matrix products, arithmetic and copies ran while one was open for 2% of the time, Pallas kernels for 10%

profile of v3, /device:TPU:0, one launch (start us, length us, event | category | flops | bytes accessed | tf_op | source)
XLA Modules:
  0.0 247.6 jit_solution(12103951407158943410)
XLA Ops:
  7.2 0.0 copy-start
  7.2 0.0 all-gather.6.cloned.1.call-start
  7.2 0.8 fusion.11
  8.0 0.2 reduce_window_sum.11
  8.2 0.8 select_reduce_fusion.1
  9.1 0.7 fusion.14
  9.7 1.6 pad_maximum_fusion.1
  11.3 0.0 all-gather.6.cloned.1.call-update
  11.3 0.0 all-gather.4.cloned.1.call-start
  11.4 25.5 %all-gather.6.cloned.1.call-done = bf16[1152,512]{1,0:T(8,128)(2,1)} async-done(((bf16[144,512]{1,0:T(8,128)(2,1)}), bf16[1152,512]{1,0:T(8,128)(2,1)}) %all-gather.6.cloned.1.call-update) | async-done | bytes 1179664 | tf_op jit(solution)/shard_map/all_gather | solution.py:378
  36.8 1.3 slice.24
  38.2 0.0 all-gather.4.cloned.1.call-update
  38.2 0.0 copy-done
  38.2 1.8 convolution_convert_fusion
  40.0 4.4 %all-to-all-start = ((bf16[4,48,4096]{2,1,0:T(8,128)(2,1)}), bf16[4,48,4096]{2,1,0:T(8,128)(2,1)}, u32[]{:S(2)}, u32[]{:S(2)}) async-start(bf16[4,48,4096]{2,1,0:T(8,128)(2,1)} %bitcast.36), calls=%async_computation | async-start | bytes 3145728 | tf_op jit(solution)/shard_map/all_to_all | solution.py:394
  44.4 20.0 %all-to-all-done = bf16[4,48,4096]{2,1,0:T(8,128)(2,1)} async-done(((bf16[4,48,4096]{2,1,0:T(8,128)(2,1)}), bf16[4,48,4096]{2,1,0:T(8,128)(2,1)}, u32[]{:S(2)}, u32[]{:S(2)}) %all-to-all-start) | async-done | bytes 1572896 | tf_op jit(solution)/shard_map/all_to_all | solution.py:394
  64.4 38.6 %all-gather.4.cloned.1.call-done = bf16[768,4096]{1,0:T(8,128)(2,1)} async-done(((bf16[768,512]{1,0:T(8,128)(2,1)}), bf16[768,4096]{1,0:T(8,128)(2,1)}) %all-gather.4.cloned.1.call-update) | async-done | bytes 6291472 | tf_op jit(solution)/shard_map/all_gather | solution.py:386
  103.0 0.0 copy-start.2
  103.0 6.5 %fusion.4 = (bf16[192]{0:T(256)(128)(2,1)S(1)}, bf16[192,768]{1,0:T(8,128)(2,1)S(1)}, bf16[192,768]{1,0:T(8,128)(2,1)}) fusion(bf16[192,1536]{1,0:T(8,128)(2,1)} %bitcast.48, bf16[192,4096]{1,0:T(8,128)(2,1)} %bitcast.3, bf16[768,4096]{1,0:T(8,128)(2,1)} %all-gather.4.cloned.1.call-done), kind=kOutput, calls=%fused_computation.10 | convolution fusion | flops 1210466048 | bytes 9044352 | tf_op jit(solution)/shard_map/dot_general | solution.py:408
  109.5 0.7 convert_element_type.75
  110.2 3.7 %all-to-all-start.1 = ((bf16[4,1,48]{2,1,0:T(2,128)(2,1)}), bf16[4,1,48]{2,1,0:T(2,128)(2,1)S(1)}, u32[]{:S(2)}, u32[]{:S(2)}) async-start(bf16[4,1,48]{2,1,0:T(2,128)(2,1)} %convert_element_type.75), calls=%async_computation.1 | async-start | bytes 4096 | tf_op jit(solution)/shard_map/all_to_all | solution.py:423
  113.8 0.0 copy-done.2
  113.8 0.0 copy-start.3
  113.8 1.2 copy-done.3
  115.0 0.0 copy-start.4
  115.0 1.2 copy-done.4
  116.3 24.3 %shard_map.129 = (bf16[128,4096]{1,0:T(8,128)(2,1)}, bf16[1024,512]{1,0:T(8,128)(2,1)}) custom-call(s32[1]{0:T(128)} %bitcast.9.pos_ref, bf16[128,4096]{1,0:T(8,128)(2,1)S(1)} %bitcast.33, bf16[128,4096]{1,0:T(8,128)(2,1)S(1)} %bitcast.34, bf16[128,4096]{1,0:T(8,128)(2,1)S(1)} %bitcast.35, bf16[1024,512]{1,0:T(8,128)(2,1)S(1)} %bitcast.30), custom_call_target="tpu_custom_call" | custom-call | flops 5368709120 | bytes 7340032 | tf_op jit(solution)/shard_map/pallas_call | solution.py:81
  140.6 0.0 copy-start.6
  140.6 0.0 all-to-all-done.1
  140.6 3.7 %all-to-all-start.2 = ((bf16[8,128,512]{2,1,0:T(8,128)(2,1)}), bf16[8,128,512]{2,1,0:T(8,128)(2,1)S(1)}, u32[]{:S(2)}, u32[]{:S(2)}) async-start(bf16[8,128,512]{2,1,0:T(8,128)(2,1)} %bitcast.13), calls=%async_computation.2 | async-start | bytes 2097152 | tf_op jit(solution)/shard_map/all_to_all | solution.py:400
  144.3 0.0 copy-done.6
  144.3 0.1 copy.21.gate_ref
  144.5 0.7 slice_convert_fusion
  145.2 0.1 fusion.10.pick_ref
  145.3 1.0 pad_maximum_fusion.pre_ref
  146.4 0.1 reshape.86
  146.4 24.4 %all-to-all-done.2 = bf16[8,128,512]{2,1,0:T(8,128)(2,1)S(1)} async-done(((bf16[8,128,512]{2,1,0:T(8,128)(2,1)}), bf16[8,128,512]{2,1,0:T(8,128)(2,1)S(1)}, u32[]{:S(2)}, u32[]{:S(2)}) %all-to-all-start.2) | async-done | bytes 1048608 | tf_op jit(solution)/shard_map/all_to_all | solution.py:400
  170.8 0.0 copy-start.5
  170.8 1.0 copy-done.5
  171.8 0.0 copy-start.1
  171.8 1.4 copy-done.1
  173.2 63.9 %shard_map.130 = bf16[128,4096]{1,0:T(8,128)(2,1)S(1)} custom-call(bf16[192,1536]{1,0:T(8,128)(2,1)S(1)} %pad_maximum_fusion.pre_ref, bf16[512,1536]{1,0:T(8,128)(2,1)S(1)} %bitcast.32, bf16[4,128,192]{2,1,0:T(8,128)(2,1)S(1)} %fusion.10.pick_ref, f32[128,1]{1,0:T(8,128)S(1)} %copy.21.gate_ref), custom_call_target="tpu_custom_call" | custom-call | flops 2415919104 | bytes 4325376 | tf_op jit(solution)/shard_map/pallas_call | solution.py:311
  237.2 0.6 select_reduce_fusion
  237.8 2.1 reduce_sum.42
  239.8 1.0 copy.23
  (5 shorter events, 0.0 us)
Async XLA Ops:
  7.2 31.0 %copy-start = (bf16[1,128,4096]{2,1,0:T(8,128)(2,1)S(1)}, bf16[1,128,4096]{2,1,0:T(8,128)(2,1)}, u32[]{:S(2)}) copy-start(bf16[1,128,4096]{2,1,0:T(8,128)(2,1)} %param.10) | copy-start | bytes 3145732
  7.2 29.7 %all-gather.6.cloned.1.call-start = ((), (), s32[]{:S(2)}) async-start(), calls=%async_computation.4 | async-start | bytes 1327104 | tf_op jit(solution)/shard_map/all_gather | solution.py:378
  11.3 91.6 %all-gather.4.cloned.1.call-start = ((), (), s32[]{:S(2)}) async-start(), calls=%async_computation.3 | async-start | bytes 7077888 | tf_op jit(solution)/shard_map/all_gather | solution.py:386
  40.0 24.4 %all-to-all-start = ((bf16[4,48,4096]{2,1,0:T(8,128)(2,1)}), bf16[4,48,4096]{2,1,0:T(8,128)(2,1)}, u32[]{:S(2)}, u32[]{:S(2)}) async-start(bf16[4,48,4096]{2,1,0:T(8,128)(2,1)} %bitcast.36), calls=%async_computation | async-start | bytes 3145728 | tf_op jit(solution)/shard_map/all_to_all | solution.py:394
  103.0 10.8 %copy-start.2 = (bf16[1,128,4096]{2,1,0:T(8,128)(2,1)S(1)}, bf16[1,128,4096]{2,1,0:T(8,128)(2,1)}, u32[]{:S(2)}) copy-start(bf16[1,128,4096]{2,1,0:T(8,128)(2,1)} %param.16) | copy-start | bytes 3145732
  110.2 30.5 %all-to-all-start.1 = ((bf16[4,1,48]{2,1,0:T(2,128)(2,1)}), bf16[4,1,48]{2,1,0:T(2,128)(2,1)S(1)}, u32[]{:S(2)}, u32[]{:S(2)}) async-start(bf16[4,1,48]{2,1,0:T(2,128)(2,1)} %convert_element_type.75), calls=%async_computation.1 | async-start | bytes 4096 | tf_op jit(solution)/shard_map/all_to_all | solution.py:423
  113.8 1.2 copy-start.3
  115.0 1.2 copy-start.4
  140.6 3.7 %copy-start.6 = (f32[1,128,1]{1,2,0:T(1,128)S(1)}, f32[1,128,1]{1,2,0:T(1,128)}, u32[]{:S(2)}) copy-start(f32[1,128,1]{1,2,0:T(1,128)} %param.12) | copy-start | bytes 1540
  140.6 30.2 %all-to-all-start.2 = ((bf16[8,128,512]{2,1,0:T(8,128)(2,1)}), bf16[8,128,512]{2,1,0:T(8,128)(2,1)S(1)}, u32[]{:S(2)}, u32[]{:S(2)}) async-start(bf16[8,128,512]{2,1,0:T(8,128)(2,1)} %bitcast.13), calls=%async_computation.2 | async-start | bytes 2097152 | tf_op jit(solution)/shard_map/all_to_all | solution.py:400
  170.8 1.0 copy-start.5
  171.8 1.4 copy-start.1
Sparse Core Ops, SparseCore 0:
  11.5 25.3 all-gather.5
  38.4 64.4 all-gather.3

commit v4 on v3

--- a/solution.py
+++ b/solution.py
@@ -13,97 +13,388 @@
 NT = (((1,), (1,)), ((), ()))
 
 
-def attention_kernel(
-    pairs, pos_ref, q_ref, g_ref, o_ref, kv_ref, dq_ref, out_ref, dkv_ref, kt_ref, bias_ref, st_ref, ds_ref
+MESH = pl.DeviceIdType.MESH
+
+
+def gather_kernel(
+    chips,
+    experts,
+    kv_ref,
+    down_ref,
+    rows_ref,
+    q_ref,
+    g_ref,
+    o_ref,
+    dq_ref,
+    kv_grad_ref,
+    hidden_ref,
+    extra_ref,
+    kv_buf,
+    down_buf,
+    row_buf,
+    kv_all,
+    terms,
+    keys_t,
+    bias,
+    scores,
+    low_grads,
+    pair_terms,
+    leaving,
+    landed,
+    kv_up,
+    kv_down,
+    kv_in,
+    kv_swap_out,
+    kv_swap_in,
+    w_up,
+    w_down,
+    w_in,
+    w_swap_out,
+    w_swap_in,
+    row_out,
+    row_in,
+    pair_out,
+    pair_in,
+    term_out,
+    term_in,
 ):
-    seq_len = kv_ref.shape[0]
-    rows = q_ref.shape[0]
+    me = lax.axis_index("ctx")
+    mine = lax.axis_index("exp")
+    z = lax.div(me, 2)
+    core = lax.rem(me, 2)
+    partner = 2 * z + 1 - core
+    tok_rows, width = q_ref.shape
+    seq_len = kv_all.shape[0]
     hd = HEAD_SIZE
+    has_up = z + 1 < chips
+    has_down = z > 0
+
+    barrier = pltpu.get_barrier_semaphore()
+    for d in range(1, chips):
+        chip = lax.rem(z + d, chips)
+        pl.semaphore_signal(
+            barrier, inc=1, device_id={"ctx": 2 * chip + core}, device_id_type=MESH
+        )
+    for d in range(1, experts):
+        pl.semaphore_signal(
+            barrier, inc=1, device_id={"exp": lax.rem(mine + d, experts)}, device_id_type=MESH
+        )
+    pl.semaphore_signal(barrier, inc=1, device_id={"ctx": partner}, device_id_type=MESH)
+    kv_buf[z, core] = kv_ref[...]
+    down_buf[z, core] = down_ref[...]
+    pl.semaphore_wait(barrier, chips + experts - 1)
+
+    def remote(src, dst, send, recv, device):
+        return pltpu.make_async_remote_copy(
+            src_ref=src,
+            dst_ref=dst,
+            send_sem=send,
+            recv_sem=recv,
+            device_id=device,
+            device_id_type=MESH,
+        )
+
+    class Line:
+        def __init__(self, buf, up, down, arrived, swap_out, swap_in):
+            self.buf, self.sems = buf, (up, down, arrived, swap_out, swap_in)
+
+        def up(self, b):
+            ref = self.buf.at[b, core]
+            return remote(ref, ref, self.sems[0].at[b], self.sems[2].at[b], {"ctx": me + 2})
+
+        def down(self, b):
+            ref = self.buf.at[b, core]
+            return remote(ref, ref, self.sems[1].at[b], self.sems[2].at[b], {"ctx": me - 2})
+
+        def swap(self, b, side):
+            ref = self.buf.at[b, side]
+            return remote(ref, ref, self.sems[3].at[b], self.sems[4].at[b], {"ctx": partner})
+
+        def begin(self):
+            @pl.when(has_up)
+            def _():
+                self.up(z).start()
+
+            @pl.when(has_down)
+            def _():
+                self.down(z).start()
+
+            self.swap(z, core).start()
+
+        def relay(self, i, on=True):
+            lo = z - i
+            hi = z + i
+
+            @pl.when((lo >= 0) & on)
+            def _():
+                self.up(lo).wait_recv()
+
+                @pl.when(has_up)
+                def _():
+                    self.up(lo).start()
+
+                self.swap(lo, core).start()
+
+            @pl.when((hi < chips) & on)
+            def _():
+                self.down(hi).wait_recv()
+
+                @pl.when(has_down)
+                def _():
+                    self.down(hi).start()
+
+                self.swap(hi, core).start()
+
+        def finish(self):
+            for b in range(chips):
+
+                @pl.when(has_up & (z >= b))
+                def _():
+                    self.up(b).wait_send()
+
+                @pl.when(has_down & (z <= b))
+                def _():
+                    self.down(b).wait_send()
+
+                self.swap(b, core).wait_send()
+
+    kv_line = Line(kv_buf, kv_up, kv_down, kv_in, kv_swap_out, kv_swap_in)
+    w_line = Line(down_buf, w_up, w_down, w_in, w_swap_out, w_swap_in)
+
+    def cross(to, slot):
+        return remote(
+            rows_ref.at[to], row_buf.at[slot], row_out.at[to], row_in.at[slot], {"exp": to}
+        )
+
+    kv_line.begin()
+    w_line.begin()
+    for d in range(1, experts):
+        cross(lax.rem(mine + d, experts), mine).start()
+    row_buf[mine] = rows_ref[mine]
+
+    terms[...] = jnp.zeros_like(terms)
+    key_pos = lax.broadcasted_iota(jnp.int32, bias.shape, 0)
+    row_pos = me * tok_rows + lax.rem(lax.broadcasted_iota(jnp.int32, bias.shape, 1), tok_rows)
+    bias[...] = jnp.where(key_pos <= row_pos, 0.0, -1e30).astype(jnp.float32)
+    for i in range(1, chips):
+        kv_line.relay(i)
+    for b in range(chips):
+        kv_line.swap(b, 1 - core).wait_recv()
+        for side in range(2):
+            kv_all[pl.ds((2 * b + side) * tok_rows, tok_rows), :] = kv_buf[b, side, :tok_rows, :]
+        extra_ref[b] = kv_buf[b, core, tok_rows:, :]
+    for head in range(KEY_VALUE_HEADS):
+        keys = kv_all[:, 2 * hd * head : 2 * hd * head + hd]
+        keys_t[head] = keys.astype(jnp.float32).T.astype(jnp.bfloat16)
+
     scale = hd**-0.5
     chunk = 256
     chunks = [pl.ds(i * chunk, chunk) for i in range(seq_len // chunk)]
-
-    @pl.when(pl.program_id(1) == 0)
-    def _():
-        kt_ref[...] = kv_ref[:, :hd].astype(jnp.float32).T.astype(jnp.bfloat16)
-        dkv_ref[...] = jnp.zeros_like(dkv_ref)
-        key_pos = lax.broadcasted_iota(jnp.int32, bias_ref.shape, 0)
-        row_pos = pos_ref[0] + lax.broadcasted_iota(jnp.int32, bias_ref.shape, 1) % rows
-        bias_ref[...] = jnp.where(key_pos <= row_pos, 0.0, -1e30).astype(jnp.float32)
-
-    for pair in range(pairs):
-        cols = [pl.ds((2 * pair + i) * hd, hd) for i in range(2)]
-        q2 = jnp.concatenate([q_ref[:, col] for col in cols], axis=0)
-        g2 = jnp.concatenate([g_ref[:, col] for col in cols], axis=0)
-        o2 = jnp.concatenate([o_ref[:, col] for col in cols], axis=0)
-        prod = g2.astype(jnp.float32) * o2.astype(jnp.float32)
-        delta = jnp.sum(prod.T, axis=0, keepdims=True)
-        top = jnp.full((1, 2 * rows), -jnp.inf, jnp.float32)
-        for part in chunks:
-            s = lax.dot_general(kv_ref[part, :hd], q2, NT, preferred_element_type=jnp.float32)
-            s = s + bias_ref[part, :]
-            st_ref[pair, part, :] = s
-            top = jnp.maximum(top, jnp.max(s, axis=0, keepdims=True))
-        total = jnp.zeros((1, 2 * rows), jnp.float32)
-        for part in chunks:
-            e = jnp.exp2((st_ref[pair, part, :] - top) * (scale * LOG2E))
-            st_ref[pair, part, :] = e
-            total = total + jnp.sum(e, axis=0, keepdims=True)
-        inverse = 1.0 / total
-        for part in chunks:
-            p = st_ref[pair, part, :] * inverse
-            dkv_ref[part, hd:] += jnp.dot(
-                p.astype(jnp.bfloat16), g2, preferred_element_type=jnp.float32
-            )
-            dp = lax.dot_general(kv_ref[part, hd:], g2, NT, preferred_element_type=jnp.float32)
-            ds = (p * (dp - delta)).astype(jnp.bfloat16)
-            ds_ref[pair, part, :] = ds
-            dkv_ref[part, :hd] += jnp.dot(ds, q2, preferred_element_type=jnp.float32) * scale
-        dqt = jnp.dot(kt_ref[...], ds_ref[pair], preferred_element_type=jnp.float32) * scale
-        dq = dqt.T
-        for i in range(2):
-            dq_ref[:, cols[i]] = dq[i * rows : (i + 1) * rows].astype(dq_ref.dtype)
-
-    @pl.when(pl.program_id(1) == pl.num_programs(1) - 1)
-    def _():
-        out_ref[...] = dkv_ref[...].astype(out_ref.dtype)
-
-
-def attention(q, g, o, kv, first):
-    rows, width = q.shape
-    seq_len = kv.shape[0]
+    pairs = scores.shape[0]
+    step = 2 * pairs * hd
+    units = width // step
+
+    def unit(u, carry):
+        for i in range(1, min(chips, 3)):
+
+            @pl.when(u == (units - 2) * (i - 1) + 1)
+            def _():
+                w_line.relay(i)
+
+        head = lax.div(u, units // KEY_VALUE_HEADS)
+        key_cols = pl.ds(pl.multiple_of(head * 2 * hd, hd), hd)
+        val_cols = pl.ds(pl.multiple_of(head * 2 * hd + hd, hd), hd)
+        for pair in range(pairs):
+            cols = [
+                pl.ds(pl.multiple_of(u * step + (2 * pair + i) * hd, hd), hd) for i in range(2)
+            ]
+            q2 = jnp.concatenate([q_ref[:, col] for col in cols], axis=0)
+            g2 = jnp.concatenate([g_ref[:, col] for col in cols], axis=0)
+            o2 = jnp.concatenate([o_ref[:, col] for col in cols], axis=0)
+            prod = g2.astype(jnp.float32) * o2.astype(jnp.float32)
+            delta = jnp.sum(prod.T, axis=0, keepdims=True)
+            top = jnp.full((1, 2 * tok_rows), -jnp.inf, jnp.float32)
+            for part in chunks:
+                s = lax.dot_general(
+                    kv_all[part, key_cols], q2, NT, preferred_element_type=jnp.float32
+                )
+                s = s + bias[part, :]
+                scores[pair, part, :] = s
+                top = jnp.maximum(top, jnp.max(s, axis=0, keepdims=True))
+            total = jnp.zeros((1, 2 * tok_rows), jnp.float32)
+            for part in chunks:
+                e = jnp.exp2((scores[pair, part, :] - top) * (scale * LOG2E))
+                scores[pair, part, :] = e
+                total = total + jnp.sum(e, axis=0, keepdims=True)
+            inverse = 1.0 / total
+            for part in chunks:
+                p = scores[pair, part, :] * inverse
+                terms[part, val_cols] += jnp.dot(
+                    p.astype(jnp.bfloat16), g2, preferred_element_type=jnp.float32
+                )
+                dp = lax.dot_general(
+                    kv_all[part, val_cols], g2, NT, preferred_element_type=jnp.float32
+                )
+                ds = (p * (dp - delta)).astype(jnp.bfloat16)
+                low_grads[pair, part, :] = ds
+                terms[part, key_cols] += (
+                    jnp.dot(ds, q2, preferred_element_type=jnp.float32) * scale
+                )
+            dq = (
+                jnp.dot(keys_t[head], low_grads[pair], preferred_element_type=jnp.float32) * scale
+            ).T
+            for i in range(2):
+                dq_ref[:, cols[i]] = dq[i * tok_rows : (i + 1) * tok_rows].astype(dq_ref.dtype)
+        return carry
+
+    lax.fori_loop(0, units, unit, 0)
+
+    def rows_of(b, side):
+        return pl.ds(pl.multiple_of((2 * b + side) * tok_rows, tok_rows), tok_rows)
+
+    def pair_copy(b, side):
+        return remote(
+            terms.at[rows_of(b, side), :],
+            pair_terms.at[b],
+            pair_out.at[b],
+            pair_in.at[b],
+            {"ctx": partner},
+        )
+
+    def term_copy(b, slot):
+        return remote(
+            leaving.at[b],
+            landed.at[slot],
+            term_out.at[b],
+            term_in.at[slot],
+            {"ctx": 2 * b + core},
+        )
+
+    for b in range(chips):
+
+        @pl.when(b <= z)
+        def _():
+            pair_copy(b, 1 - core).start()
+
+    for d in range(1, experts):
+        j = lax.rem(mine + d, experts)
+        cross(j, j).wait_recv()
+    hidden_ref[...] = jnp.zeros_like(hidden_ref)
+    shard = down_ref.shape[1]
+    tile = 256
+    slots = hidden_ref.shape[0]
+
+    def hidden_part(i):
+        w_line.relay(i, i >= 3)
+        ahead = lax.rem(z + i, chips)
+        behind = lax.rem(z - i + chips, chips)
+        b = jnp.where(z < chips // 2, ahead, behind)
+        w_line.swap(b, 1 - core).wait_recv()
+        for side in range(2):
+            cols = pl.ds(pl.multiple_of((2 * b + side) * shard, shard), shard)
+            rows = row_buf[:, :, cols].reshape(slots, shard)
+            for t in range(hidden_ref.shape[1] // tile):
+                part = pl.ds(t * tile, tile)
+                hidden_ref[:, part] += lax.dot_general(
+                    rows, down_buf[b, side, part, :], NT, preferred_element_type=jnp.float32
+                )
+
+    def hidden_turn(i, carry):
+        hidden_part(i)
+        return carry
+
+    lax.fori_loop(0, chips - 1, hidden_turn, 0)
+
+    for b in range(chips):
+
+        @pl.when(b <= z)
+        def _():
+            pair_copy(b, core).wait_recv()
+
+        @pl.when(b < z)
+        def _():
+            leaving[b] = (terms[rows_of(b, core), :] + pair_terms[b]).astype(leaving.dtype)
+            term_copy(b, z).start()
+
+    hidden_part(chips - 1)
+
+    landed_sum = terms[rows_of(z, core), :] + pair_terms[z]
+    kv_sum = pair_terms.at[z]
+    kv_sum[...] = landed_sum
+    for b in range(chips):
+
+        @pl.when(b > z)
+        def _():
+            term_copy(b, b).wait_recv()
+            kv_sum[...] += landed[b].astype(jnp.float32)
+
+    kv_grad_ref[...] = kv_sum[...].astype(kv_grad_ref.dtype)
+
+    kv_line.finish()
+    w_line.finish()
+    for d in range(1, experts):
+        cross(lax.rem(mine + d, experts), mine).wait_send()
+    for b in range(chips):
+
+        @pl.when(b <= z)
+        def _():
+            pair_copy(b, 1 - core).wait_send()
+
+        @pl.when(b < z)
+        def _():
+            term_copy(b, z).wait_send()
+
+
+def gather_and_attend(kv_local, down, rows, q, g, o, chips):
+    experts, capacity, width = rows.shape
+    tok_rows = q.shape[0]
+    kv_width = kv_local.shape[1]
+    contexts = 2 * chips
+    seq_len = contexts * tok_rows
+    hidden = down.shape[0]
     hd = HEAD_SIZE
     pairs = 2
-    step = pairs * 2 * hd
-    steps = width // KEY_VALUE_HEADS // step
-    tok = pl.BlockSpec((rows, step), lambda h, i: (0, h * steps + i))
-    key = pl.BlockSpec((seq_len, 2 * hd), lambda h, i: (0, h))
+    vmem = pl.BlockSpec(memory_space=pltpu.VMEM)
+    low, full = jnp.bfloat16, jnp.float32
+    dma = pltpu.SemaphoreType.DMA
+    per_chip = dma((chips,))
+    extra = kv_local.shape[0] - tok_rows
     return pl.pallas_call(
-        functools.partial(attention_kernel, pairs),
-        grid=(KEY_VALUE_HEADS, steps),
-        in_specs=[pl.BlockSpec(memory_space=pltpu.SMEM), tok, tok, tok, key],
-        out_specs=[tok, key],
+        functools.partial(gather_kernel, chips, experts),
+        in_specs=[vmem] * 6,
+        out_specs=[vmem] * 4,
         out_shape=[
-            jax.ShapeDtypeStruct((rows, width), jnp.bfloat16),
-            jax.ShapeDtypeStruct((seq_len, kv.shape[1]), jnp.bfloat16),
+            jax.ShapeDtypeStruct((tok_rows, width), low),
+            jax.ShapeDtypeStruct((tok_rows, kv_width), low),
+            jax.ShapeDtypeStruct((experts * capacity, hidden), full),
+            jax.ShapeDtypeStruct((chips, extra, kv_width), low),
         ],
         scratch_shapes=[
-            pltpu.VMEM((seq_len, 2 * hd), jnp.float32),
-            pltpu.VMEM((hd, seq_len), jnp.bfloat16),
-            pltpu.VMEM((seq_len, 2 * rows), jnp.float32),
-            pltpu.VMEM((pairs, seq_len, 2 * rows), jnp.float32),
-            pltpu.VMEM((pairs, seq_len, 2 * rows), jnp.bfloat16),
-        ],
-        compiler_params=pltpu.CompilerParams(vmem_limit_bytes=40 * 1024 * 1024),
+            pltpu.VMEM((chips, 2) + kv_local.shape, low),
+            pltpu.VMEM((chips, 2) + down.shape, low),
+            pltpu.VMEM((experts, capacity, width), low),
+            pltpu.VMEM((seq_len, kv_width), low),
+            pltpu.VMEM((seq_len, kv_width), full),
+            pltpu.VMEM((KEY_VALUE_HEADS, hd, seq_len), low),
+            pltpu.VMEM((seq_len, 2 * tok_rows), full),
+            pltpu.VMEM((pairs, seq_len, 2 * tok_rows), full),
+            pltpu.VMEM((pairs, seq_len, 2 * tok_rows), low),
+            pltpu.VMEM((chips, tok_rows, kv_width), full),
+            pltpu.VMEM((chips, tok_rows, kv_width), low),
+            pltpu.VMEM((chips, tok_rows, kv_width), low),
+        ]
+        + [per_chip] * 10
+        + [dma((experts,))] * 2
+        + [per_chip] * 4,
+        compiler_params=pltpu.CompilerParams(
+            collective_id=1, has_side_effects=True, vmem_limit_bytes=52 * 1024 * 1024
+        ),
         cost_estimate=pl.CostEstimate(
-            flops=10 * rows * seq_len * width,
-            bytes_accessed=8 * rows * width + 6 * seq_len * kv.shape[1],
-            transcendentals=rows * seq_len * width // hd,
+            flops=10 * tok_rows * seq_len * width,
+            bytes_accessed=8 * tok_rows * width,
+            transcendentals=tok_rows * seq_len * width // hd,
         ),
-    )(first, q, g, o, kv)
-
-
-MESH = pl.DeviceIdType.MESH
+    )(kv_local, down, rows, q, g, o)
 
 
 def return_kernel(
@@ -375,15 +666,7 @@
     extra = jnp.broadcast_to(
         jnp.pad(slot_keys.astype(jnp.bfloat16), (0, kv_width - tok_rows))[None], (16, kv_width)
     )
-    kv_wide = lax.all_gather(jnp.concatenate([kv_local, extra], axis=0), "ctx", axis=0)
-    kv_all = kv_wide[:, :tok_rows].reshape(contexts * tok_rows, kv_width)
-    block_keys = kv_wide[:, tok_rows, :tok_rows].astype(jnp.int32)
-    core = lax.axis_index("ctx") % 2
-    block_keys = block_keys.reshape(chips, 2, tok_rows)
-    block_keys = jnp.where(core == 0, block_keys[:, 0], block_keys[:, 1])
-
-    down_shard, kv_all = lax.optimization_barrier((down_weight[0], kv_all))
-    down_full = lax.all_gather(down_shard, "ctx", axis=1, tiled=True)
+    kv_wide = jnp.concatenate([kv_local, extra], axis=0)
 
     dispatch = (jnp.arange(slots, dtype=jnp.int32)[:, None] == slot_keys[None, :]).astype(
         jnp.bfloat16
@@ -391,21 +674,17 @@
     send_rows = jnp.dot(dispatch, grad_out[0], preferred_element_type=jnp.float32).astype(
         jnp.bfloat16
     )
-    expert_rows = lax.all_to_all(
-        send_rows.reshape(experts, capacity, width), "exp", split_axis=0, concat_axis=0, tiled=True
-    ).reshape(slots, width)
-
-    first = (lax.axis_index("ctx") * tok_rows).astype(jnp.int32).reshape(1)
-    query_grad, kv_terms = attention(queries[0], attn_grad[0], attn_out[0], kv_all, first)
-    kv_back = lax.all_to_all(
-        kv_terms.reshape(contexts, tok_rows, kv_width),
-        "ctx",
-        split_axis=0,
-        concat_axis=0,
-        tiled=True,
+    query_grad, kv_grad, down_grad, block_extra = gather_and_attend(
+        kv_wide,
+        down_weight[0],
+        send_rows.reshape(experts, capacity, width),
+        queries[0],
+        attn_grad[0],
+        attn_out[0],
+        chips,
     )
-
-    down_grad = lax.dot_general(expert_rows, down_full, NT, preferred_element_type=jnp.float32)
+    block_keys = block_extra[:, 0, :tok_rows].astype(jnp.int32)
+
     pre_acts = saved_pre[0, 0]
     if capacity != filled:
         pre_acts = pre_acts.reshape(experts, filled, 2 * hidden)
@@ -423,7 +702,6 @@
     back_prob = lax.all_to_all(
         slot_prob.reshape(experts, capacity), "exp", split_axis=0, concat_axis=0, tiled=True
     ).reshape(slots)
-    pre_grad, back_prob, kv_back = lax.optimization_barrier((pre_grad, back_prob, kv_back))
     pick = (block_keys[:, :, None] == jnp.arange(slots, dtype=jnp.int32)).astype(jnp.bfloat16)
     moe_input_grad = expert_return(
         pre_grad, gate_up_weight[0], pick, gate_probs[0], chips, experts
@@ -432,7 +710,6 @@
     prob_grad = jnp.sum(
         jnp.where(own_slots, back_prob.astype(jnp.float32), 0.0), axis=1
     ).astype(jnp.bfloat16)[None, :, None]
-    kv_grad = jnp.sum(kv_back.astype(jnp.float32), axis=0).astype(jnp.bfloat16)
     return (moe_input_grad, prob_grad, query_grad[None], kv_grad[None])
 
 

time: 248 us -> 162 us (0.65)
  waiting for transfers between devices: 108 us -> 0.01 us
  Pallas kernels: 88.3 us -> 147 us
  between operations: 14.2 us -> 0.78 us
  starting transfers between devices: 11.8 us -> 3.53 us
  matrix products: 8.3 us -> 1.72 us
  other arithmetic: 8.63 us -> 3.81 us
  local copies, waits for them, and re-layouts: 8.02 us -> 4.91 us
    all_gather x2 -> x0, waiting for transfers between devices: 64.1 us -> none  [the longest x1 38.6 us: body(): down_full = lax.all_gather(down_shard, 'ctx', axis=1, tiled=True)]
    pallas_call x1, Pallas kernels: 24.3 us -> 83.1 us  [gather_and_attend(): pl.pallas_call(functools.partial(gather_kernel, chips, experts), in_specs...]
    all_to_all x2 -> x0, waiting for transfers between devices: 44.4 us -> none  [the longest x1 24.4 us: body(): lax.all_to_all(kv_terms.reshape(contexts, tok_rows, kv_width), 'ctx', spl...]
    all_to_all x2 -> x0, starting transfers between devices: 8.05 us -> none  [the longest x1 4.36 us: body(): lax.all_to_all(send_rows.reshape(experts, capacity, width), 'exp', split_...]
    dot_general x1 -> x0, matrix products: 6.51 us -> none  [body(): lax.dot_general(expert_rows, down_full, NT, preferred_element_type=jnp.fl...]
    unnamed x15 -> x17, local copies, waits for them, and re-layouts: 5.81 us -> 4.03 us
  transfers between devices with their start and end apart: 5 -> 1, of which waited for: 4 -> 0; matrix products, arithmetic and copies ran while one was open for 2% -> 0% of each run, Pallas kernels for 10% -> 39%
where the time goes in v4:
time: 162 us
  Pallas kernels  147 us (91%)
  local copies, waits for them, and re-layouts  4.91 us (3%)
  other arithmetic  3.81 us (2%)
  starting transfers between devices  3.53 us (2%)
  matrix products  1.72 us (1%)
    pallas_call x1, Pallas kernels, gather_and_attend(): pl.pallas_call(functools.partial(gather_kernel, chips, experts), in_specs...  83.1 us
    pallas_call x1, Pallas kernels, expert_return(): pl.pallas_call(functools.partial(return_kernel, chips, experts), in_specs...  63.9 us
    unnamed x17, local copies, waits for them, and re-layouts  4.03 us
    all_to_all x1, starting transfers between devices, body(): lax.all_to_all(slot_prob.reshape(experts, capacity), 'exp', split_axis=0,...  3.53 us
  transfers between devices with their start and end apart: 1, of which 0 were waited for; matrix products, arithmetic and copies ran while one was open for 0% of the time, Pallas kernels for 39%

profile of v4, /device:TPU:0, one launch (start us, length us, event | category | flops | bytes accessed | tf_op | source)
XLA Modules:
  0.0 161.7 jit_solution(18312211666208393015)
XLA Ops:
  0.6 0.0 copy-start
  0.6 0.0 copy-start.5
  0.7 0.8 fusion.11
  1.5 0.0 copy-start.2
  1.5 0.2 reduce_window_sum.11
  1.7 0.9 select_reduce_fusion.1
  2.6 0.7 fusion.14
  3.2 0.0 copy-done
  3.2 1.7 %convolution_convert_fusion = bf16[192,4096]{1,0:T(8,128)(2,1)} fusion(bf16[1,128,4096]{2,1,0:T(8,128)(2,1)S(1)} %copy-done, s32[128]{0:T(128)S(1)} %get-tuple-element.13), kind=kOutput, calls=%fused_computation | convolution fusion | flops 202137600 | bytes 2621952 | tf_op jit(solution)/shard_map/dot_general | solution.py:674
  5.0 0.0 copy-done.5
  5.0 0.0 copy-done.2
  5.0 0.0 copy-start.4
  5.0 83.1 %shard_map.129 = (bf16[128,4096]{1,0:T(8,128)(2,1)}, bf16[128,512]{1,0:T(8,128)(2,1)S(1)}, f32[192,768]{1,0:T(8,128)S(1)}, bf16[4,16,512]{2,1,0:T(8,128)(2,1)S(1)}) custom-call(bf16[144,512]{1,0:T(8,128)(2,1)S(1)} %pad_maximum_fusion.1.kv_ref, bf16[768,512]{1,0:T(8,128)(2,1)S(1)} %bitcast.25, bf16[4,48,4096]{2,1,0:T(8,128)(2,1)} %bitcast.26, ...), custom_call_target="tpu_custom_call" | custom-call | flops 5368709120 | bytes 4194304 | tf_op jit(solution)/shard_map/pallas_call | solution.py:362
  88.1 0.0 copy-start.6
  88.1 0.0 copy-done.4
  88.1 0.4 fusion.4
  88.5 0.7 convert_element_type.81
  89.2 3.5 %all-to-all-start = ((bf16[4,1,48]{2,1,0:T(2,128)(2,1)}), bf16[4,1,48]{2,1,0:T(2,128)(2,1)S(1)}, u32[]{:S(2)}, u32[]{:S(2)}) async-start(bf16[4,1,48]{2,1,0:T(2,128)(2,1)} %convert_element_type.81), calls=%async_computation | async-start | bytes 4096 | tf_op jit(solution)/shard_map/all_to_all | solution.py:702
  92.7 0.1 fusion.10.pick_ref
  92.9 0.0 copy-done.6
  92.9 0.1 copy.18.gate_ref
  93.0 0.0 copy-start.1
  93.0 1.4 copy-done.1
  94.4 63.9 %shard_map.130 = bf16[128,4096]{1,0:T(8,128)(2,1)S(1)} custom-call(bf16[192,1536]{1,0:T(8,128)(2,1)S(1)} %pad_maximum_fusion.pre_ref, bf16[512,1536]{1,0:T(8,128)(2,1)S(1)} %bitcast.24, bf16[4,128,192]{2,1,0:T(8,128)(2,1)S(1)} %fusion.10.pick_ref, f32[128,1]{1,0:T(8,128)S(1)} %copy.18.gate_ref), custom_call_target="tpu_custom_call" | custom-call | flops 2415919104 | bytes 4325376 | tf_op jit(solution)/shard_map/pallas_call | solution.py:602
  158.3 0.0 copy-start.3
  158.3 0.0 all-to-all-done
  158.4 0.1 reshape.65
  158.5 0.6 select_reduce_fusion
  159.1 1.0 copy.23
  160.0 0.0 copy-done.3
  160.0 1.0 copy.24
  161.0 0.7 copy.25
  (6 shorter events, 0.1 us)
Async XLA Ops:
  0.6 2.6 %copy-start = (bf16[1,128,4096]{2,1,0:T(8,128)(2,1)S(1)}, bf16[1,128,4096]{2,1,0:T(8,128)(2,1)}, u32[]{:S(2)}) copy-start(bf16[1,128,4096]{2,1,0:T(8,128)(2,1)} %param.10) | copy-start | bytes 3145732
  0.6 4.3 %copy-start.5 = (bf16[1,128,512]{2,1,0:T(8,128)(2,1)S(1)}, bf16[1,128,512]{2,1,0:T(8,128)(2,1)}, u32[]{:S(2)}) copy-start(bf16[1,128,512]{2,1,0:T(8,128)(2,1)} %param.17) | copy-start | bytes 393220
  1.5 3.5 %copy-start.2 = (bf16[1,768,512]{2,1,0:T(8,128)(2,1)S(1)}, bf16[1,768,512]{2,1,0:T(8,128)(2,1)}, u32[]{:S(2)}) copy-start(bf16[1,768,512]{2,1,0:T(8,128)(2,1)} %param.14) | copy-start | bytes 2359300
  5.0 83.1 %copy-start.4 = (bf16[1,1,192,1536]{3,2,1,0:T(8,128)(2,1)S(1)}, bf16[1,1,192,1536]{3,2,1,0:T(8,128)(2,1)}, u32[]{:S(2)}) copy-start(bf16[1,1,192,1536]{3,2,1,0:T(8,128)(2,1)} %param.13) | copy-start | bytes 1769476
  88.1 4.8 %copy-start.6 = (f32[1,128,1]{1,2,0:T(1,128)S(1)}, f32[1,128,1]{1,2,0:T(1,128)}, u32[]{:S(2)}) copy-start(f32[1,128,1]{1,2,0:T(1,128)} %param.12) | copy-start | bytes 1540
  89.2 69.1 %all-to-all-start = ((bf16[4,1,48]{2,1,0:T(2,128)(2,1)}), bf16[4,1,48]{2,1,0:T(2,128)(2,1)S(1)}, u32[]{:S(2)}, u32[]{:S(2)}) async-start(bf16[4,1,48]{2,1,0:T(2,128)(2,1)} %convert_element_type.81), calls=%async_computation | async-start | bytes 4096 | tf_op jit(solution)/shard_map/all_to_all | solution.py:702
  93.0 1.4 copy-start.1
  158.3 1.7 %copy-start.3 = (bf16[128,4096]{1,0:T(8,128)(2,1)S(1)}, bf16[128,4096]{1,0:T(8,128)(2,1)}, u32[]{:S(2)}) copy-start(bf16[128,4096]{1,0:T(8,128)(2,1)} %get-tuple-element.10) | copy-start | bytes 3145732

commit v5 on v4

--- a/solution.py
+++ b/solution.py
@@ -10,6 +10,7 @@
 KEY_VALUE_HEADS = 2
 HEAD_SIZE = 128
 LOG2E = 1.4426950408889634
+PARTS = 2
 NT = (((1,), (1,)), ((), ()))
 
 
@@ -19,16 +20,21 @@
 def gather_kernel(
     chips,
     experts,
+    routes_ref,
     kv_ref,
     down_ref,
-    rows_ref,
+    token_ref,
+    acts_ref,
     q_ref,
     g_ref,
     o_ref,
     dq_ref,
     kv_grad_ref,
+    pre_ref,
+    prob_ref,
+    pick_ref,
+    rows_ref,
     hidden_ref,
-    extra_ref,
     kv_buf,
     down_buf,
     row_buf,
@@ -80,7 +86,28 @@
             barrier, inc=1, device_id={"exp": lax.rem(mine + d, experts)}, device_id_type=MESH
         )
     pl.semaphore_signal(barrier, inc=1, device_id={"ctx": partner}, device_id_type=MESH)
-    kv_buf[z, core] = kv_ref[...]
+    capacity = rows_ref.shape[1]
+    slots = experts * capacity
+    routes = routes_ref[...]
+    at = lax.broadcasted_iota(jnp.int32, (-(-experts // 16) * 16, tok_rows), 0)
+    named = jnp.where(at == routes, 1.0, 0.0).astype(jnp.float32)
+    row = lax.broadcasted_iota(jnp.int32, (tok_rows, tok_rows), 0)
+    col = lax.broadcasted_iota(jnp.int32, (tok_rows, tok_rows), 1)
+    before = jnp.where(row < col, 1.0, 0.0).astype(jnp.bfloat16)
+    earlier = jnp.dot(named.astype(jnp.bfloat16), before, preferred_element_type=jnp.float32)
+    place = jnp.sum(earlier * named, axis=0, keepdims=True)
+    slot_keys = routes.astype(jnp.float32) * capacity + place
+
+    def one_hot(keys):
+        at = lax.broadcasted_iota(jnp.int32, (slots, tok_rows), 0).astype(jnp.float32)
+        return jnp.where(at == keys, 1.0, 0.0).astype(jnp.float32)
+
+    extra = kv_buf.shape[2] - tok_rows
+    kv_buf[z, core, :tok_rows, :] = kv_ref[...]
+    kv_buf[z, core, tok_rows:, :] = jnp.zeros((extra, kv_ref.shape[1]), kv_buf.dtype)
+    kv_buf[z, core, tok_rows:, :tok_rows] = jnp.broadcast_to(slot_keys, (extra, tok_rows)).astype(
+        kv_buf.dtype
+    )
     down_buf[z, core] = down_ref[...]
     pl.semaphore_wait(barrier, chips + experts - 1)
 
@@ -95,71 +122,79 @@
         )
 
     class Line:
-        def __init__(self, buf, up, down, arrived, swap_out, swap_in):
+        def __init__(self, buf, parts, up, down, arrived, swap_out, swap_in):
             self.buf, self.sems = buf, (up, down, arrived, swap_out, swap_in)
-
-        def up(self, b):
-            ref = self.buf.at[b, core]
-            return remote(ref, ref, self.sems[0].at[b], self.sems[2].at[b], {"ctx": me + 2})
-
-        def down(self, b):
-            ref = self.buf.at[b, core]
-            return remote(ref, ref, self.sems[1].at[b], self.sems[2].at[b], {"ctx": me - 2})
-
-        def swap(self, b, side):
-            ref = self.buf.at[b, side]
-            return remote(ref, ref, self.sems[3].at[b], self.sems[4].at[b], {"ctx": partner})
+            self.parts, self.rows = parts, buf.shape[2] // parts
+
+        def piece(self, b, p, side):
+            return self.buf.at[b, side, pl.ds(p * self.rows, self.rows), :]
+
+        def up(self, b, p):
+            ref = self.piece(b, p, core)
+            return remote(ref, ref, self.sems[0].at[b, p], self.sems[2].at[b, p], {"ctx": me + 2})
+
+        def down(self, b, p):
+            ref = self.piece(b, p, core)
+            return remote(ref, ref, self.sems[1].at[b, p], self.sems[2].at[b, p], {"ctx": me - 2})
+
+        def swap(self, b, p, side):
+            ref = self.piece(b, p, side)
+            return remote(ref, ref, self.sems[3].at[b, p], self.sems[4].at[b, p], {"ctx": partner})
 
         def begin(self):
-            @pl.when(has_up)
-            def _():
-                self.up(z).start()
-
-            @pl.when(has_down)
-            def _():
-                self.down(z).start()
-
-            self.swap(z, core).start()
-
-        def relay(self, i, on=True):
+            for p in range(self.parts):
+
+                @pl.when(has_up)
+                def _():
+                    self.up(z, p).start()
+
+                @pl.when(has_down)
+                def _():
+                    self.down(z, p).start()
+
+            for p in range(self.parts):
+                self.swap(z, p, core).start()
+
+        def relay(self, i, p, on=True):
             lo = z - i
             hi = z + i
 
             @pl.when((lo >= 0) & on)
             def _():
-                self.up(lo).wait_recv()
+                self.up(lo, p).wait_recv()
 
                 @pl.when(has_up)
                 def _():
-                    self.up(lo).start()
-
-                self.swap(lo, core).start()
+                    self.up(lo, p).start()
+
+                self.swap(lo, p, core).start()
 
             @pl.when((hi < chips) & on)
             def _():
-                self.down(hi).wait_recv()
+                self.down(hi, p).wait_recv()
 
                 @pl.when(has_down)
                 def _():
-                    self.down(hi).start()
-
-                self.swap(hi, core).start()
+                    self.down(hi, p).start()
+
+                self.swap(hi, p, core).start()
 
         def finish(self):
             for b in range(chips):
-
-                @pl.when(has_up & (z >= b))
-                def _():
-                    self.up(b).wait_send()
-
-                @pl.when(has_down & (z <= b))
-                def _():
-                    self.down(b).wait_send()
-
-                self.swap(b, core).wait_send()
-
-    kv_line = Line(kv_buf, kv_up, kv_down, kv_in, kv_swap_out, kv_swap_in)
-    w_line = Line(down_buf, w_up, w_down, w_in, w_swap_out, w_swap_in)
+                for p in range(self.parts):
+
+                    @pl.when(has_up & (z >= b))
+                    def _():
+                        self.up(b, p).wait_send()
+
+                    @pl.when(has_down & (z <= b))
+                    def _():
+                        self.down(b, p).wait_send()
+
+                    self.swap(b, p, core).wait_send()
+
+    kv_line = Line(kv_buf, 1, kv_up, kv_down, kv_in, kv_swap_out, kv_swap_in)
+    w_line = Line(down_buf, PARTS, w_up, w_down, w_in, w_swap_out, w_swap_in)
 
     def cross(to, slot):
         return remote(
@@ -168,6 +203,15 @@
 
     kv_line.begin()
     w_line.begin()
+    dispatch = one_hot(slot_keys).astype(jnp.bfloat16)
+    wide = 512
+    for t in range(width // wide):
+        cols = pl.ds(t * wide, wide)
+        rows_ref[:, :, cols] = (
+            jnp.dot(dispatch, token_ref[:, cols], preferred_element_type=jnp.float32)
+            .astype(rows_ref.dtype)
+            .reshape(experts, capacity, wide)
+        )
     for d in range(1, experts):
         cross(lax.rem(mine + d, experts), mine).start()
     row_buf[mine] = rows_ref[mine]
@@ -177,12 +221,13 @@
     row_pos = me * tok_rows + lax.rem(lax.broadcasted_iota(jnp.int32, bias.shape, 1), tok_rows)
     bias[...] = jnp.where(key_pos <= row_pos, 0.0, -1e30).astype(jnp.float32)
     for i in range(1, chips):
-        kv_line.relay(i)
+        kv_line.relay(i, 0)
     for b in range(chips):
-        kv_line.swap(b, 1 - core).wait_recv()
+        kv_line.swap(b, 0, 1 - core).wait_recv()
         for side in range(2):
             kv_all[pl.ds((2 * b + side) * tok_rows, tok_rows), :] = kv_buf[b, side, :tok_rows, :]
-        extra_ref[b] = kv_buf[b, core, tok_rows:, :]
+        keys = kv_buf[b, core, tok_rows:, :tok_rows].astype(jnp.float32)
+        pick_ref[b] = one_hot(keys[:1]).T.astype(pick_ref.dtype)
     for head in range(KEY_VALUE_HEADS):
         keys = kv_all[:, 2 * hd * head : 2 * hd * head + hd]
         keys_t[head] = keys.astype(jnp.float32).T.astype(jnp.bfloat16)
@@ -195,11 +240,12 @@
     units = width // step
 
     def unit(u, carry):
-        for i in range(1, min(chips, 3)):
-
-            @pl.when(u == (units - 2) * (i - 1) + 1)
-            def _():
-                w_line.relay(i)
+        for when, i, p in ((0, 1, 0), (2, 1, 1), (5, 2, 0), (7, 2, 1)):
+            if i < chips:
+
+                @pl.when(u == when)
+                def _():
+                    w_line.relay(i, p)
 
         head = lax.div(u, units // KEY_VALUE_HEADS)
         key_cols = pl.ds(pl.multiple_of(head * 2 * hd, hd), hd)
@@ -281,26 +327,26 @@
         cross(j, j).wait_recv()
     hidden_ref[...] = jnp.zeros_like(hidden_ref)
     shard = down_ref.shape[1]
-    tile = 256
-    slots = hidden_ref.shape[0]
-
-    def hidden_part(i):
-        w_line.relay(i, i >= 3)
+    hidden = hidden_ref.shape[1]
+    piece = hidden // PARTS
+
+    def hidden_part(i, p):
+        w_line.relay(i, p, i >= 3)
         ahead = lax.rem(z + i, chips)
         behind = lax.rem(z - i + chips, chips)
         b = jnp.where(z < chips // 2, ahead, behind)
-        w_line.swap(b, 1 - core).wait_recv()
+        w_line.swap(b, p, 1 - core).wait_recv()
+        part = pl.ds(p * piece, piece)
         for side in range(2):
             cols = pl.ds(pl.multiple_of((2 * b + side) * shard, shard), shard)
             rows = row_buf[:, :, cols].reshape(slots, shard)
-            for t in range(hidden_ref.shape[1] // tile):
-                part = pl.ds(t * tile, tile)
-                hidden_ref[:, part] += lax.dot_general(
-                    rows, down_buf[b, side, part, :], NT, preferred_element_type=jnp.float32
-                )
+            hidden_ref[:, part] += lax.dot_general(
+                rows, down_buf[b, side, part, :], NT, preferred_element_type=jnp.float32
+            )
 
     def hidden_turn(i, carry):
-        hidden_part(i)
+        for p in range(PARTS):
+            hidden_part(i, p)
         return carry
 
     lax.fori_loop(0, chips - 1, hidden_turn, 0)
@@ -316,7 +362,26 @@
             leaving[b] = (terms[rows_of(b, core), :] + pair_terms[b]).astype(leaving.dtype)
             term_copy(b, z).start()
 
-    hidden_part(chips - 1)
+    prob = jnp.zeros((slots, 1), jnp.float32)
+    tile = 128
+    for p in range(PARTS):
+        hidden_part(chips - 1, p)
+        for t in range(p * piece, (p + 1) * piece, tile):
+            grad = hidden_ref[:, t : t + tile]
+            gate_pre = acts_ref[:, t : t + tile].astype(jnp.float32)
+            up_pre = acts_ref[:, hidden + t : hidden + t + tile].astype(jnp.float32)
+            sigma = jax.nn.sigmoid(gate_pre)
+            swish = gate_pre * sigma
+            up_part = grad * swish
+            prob = prob + jnp.sum(up_part * up_pre, axis=-1, keepdims=True)
+            gate_part = grad * up_pre * sigma * (1.0 + gate_pre * (1.0 - sigma))
+            pre_ref[:, t : t + tile] = gate_part.astype(pre_ref.dtype)
+            pre_ref[:, hidden + t : hidden + t + tile] = up_part.astype(pre_ref.dtype)
+    prob_ref[...] = (
+        jnp.broadcast_to(prob, (slots, prob_ref.shape[2]))
+        .astype(prob_ref.dtype)
+        .reshape(prob_ref.shape)
+    )
 
     landed_sum = terms[rows_of(z, core), :] + pair_terms[z]
     kv_sum = pair_terms.at[z]
@@ -345,33 +410,35 @@
             term_copy(b, z).wait_send()
 
 
-def gather_and_attend(kv_local, down, rows, q, g, o, chips):
-    experts, capacity, width = rows.shape
-    tok_rows = q.shape[0]
+def gather_and_attend(routes, kv_local, down, tokens, acts, q, g, o, chips, experts):
+    tok_rows, width = q.shape
     kv_width = kv_local.shape[1]
-    contexts = 2 * chips
-    seq_len = contexts * tok_rows
-    hidden = down.shape[0]
+    seq_len = 2 * chips * tok_rows
+    hidden, shard = down.shape
+    slots = acts.shape[0]
+    capacity = slots // experts
     hd = HEAD_SIZE
     pairs = 2
     vmem = pl.BlockSpec(memory_space=pltpu.VMEM)
     low, full = jnp.bfloat16, jnp.float32
     dma = pltpu.SemaphoreType.DMA
     per_chip = dma((chips,))
-    extra = kv_local.shape[0] - tok_rows
     return pl.pallas_call(
         functools.partial(gather_kernel, chips, experts),
-        in_specs=[vmem] * 6,
-        out_specs=[vmem] * 4,
+        in_specs=[vmem] * 8,
+        out_specs=[vmem] * 5,
         out_shape=[
             jax.ShapeDtypeStruct((tok_rows, width), low),
             jax.ShapeDtypeStruct((tok_rows, kv_width), low),
-            jax.ShapeDtypeStruct((experts * capacity, hidden), full),
-            jax.ShapeDtypeStruct((chips, extra, kv_width), low),
+            jax.ShapeDtypeStruct((slots, 2 * hidden), low),
+            jax.ShapeDtypeStruct((experts, capacity, 128), low),
+            jax.ShapeDtypeStruct((chips, tok_rows, slots), low),
         ],
         scratch_shapes=[
-            pltpu.VMEM((chips, 2) + kv_local.shape, low),
-            pltpu.VMEM((chips, 2) + down.shape, low),
+            pltpu.VMEM((experts, capacity, width), low),
+            pltpu.VMEM((slots, hidden), full),
+            pltpu.VMEM((chips, 2, tok_rows + 16, kv_width), low),
+            pltpu.VMEM((chips, 2, hidden, shard), low),
             pltpu.VMEM((experts, capacity, width), low),
             pltpu.VMEM((seq_len, kv_width), low),
             pltpu.VMEM((seq_len, kv_width), full),
@@ -383,18 +450,19 @@
             pltpu.VMEM((chips, tok_rows, kv_width), low),
             pltpu.VMEM((chips, tok_rows, kv_width), low),
         ]
-        + [per_chip] * 10
+        + [dma((chips, 1))] * 5
+        + [dma((chips, PARTS))] * 5
         + [dma((experts,))] * 2
         + [per_chip] * 4,
         compiler_params=pltpu.CompilerParams(
-            collective_id=1, has_side_effects=True, vmem_limit_bytes=52 * 1024 * 1024
+            collective_id=1, has_side_effects=True, vmem_limit_bytes=54 * 1024 * 1024
         ),
         cost_estimate=pl.CostEstimate(
             flops=10 * tok_rows * seq_len * width,
             bytes_accessed=8 * tok_rows * width,
             transcendentals=tok_rows * seq_len * width // hd,
         ),
-    )(kv_local, down, rows, q, g, o)
+    )(routes, kv_local, down, tokens, acts, q, g, o)
 
 
 def return_kernel(
@@ -404,7 +472,10 @@
     gu_ref,
     pick_ref,
     gate_ref,
+    prob_ref,
     out_ref,
+    token_prob_ref,
+    prob_buf,
     pre_buf,
     gu_buf,
     sent,
@@ -412,6 +483,8 @@
     leaving,
     landed,
     pair_sems,
+    prob_out,
+    prob_in,
     up_sems,
     down_sems,
     pre_sems,
@@ -491,8 +564,18 @@
     def _():
         down(z).start()
 
+    def prob_copy(to, slot):
+        return remote(
+            prob_ref.at[to], prob_buf.at[slot], prob_out.at[to], prob_in.at[slot], {"exp": to}
+        )
+
     swap.start()
-    gu_buf[core] = gu_ref[...]
+    keep = pltpu.make_async_copy(gu_ref, gu_buf.at[core], pair_sems.at[2])
+    keep.start()
+    for d in range(1, experts):
+        prob_copy(lax.rem(mine + d, experts), mine).start()
+    prob_buf[mine] = prob_ref[mine]
+    keep.wait()
     swap.wait_recv()
 
     def block_of(i):
@@ -571,7 +654,19 @@
             gate_ref[...] * landed[b].astype(jnp.float32)
         ).astype(out_ref.dtype)
 
+    for d in range(1, experts):
+        j = lax.rem(mine + d, experts)
+        prob_copy(j, j).wait_recv()
+    lanes = prob_ref.shape[2]
+    token_prob_ref[...] = jnp.dot(
+        pick_ref[z],
+        prob_buf[...].reshape(pick_ref.shape[2], lanes),
+        preferred_element_type=jnp.float32,
+    ).astype(token_prob_ref.dtype)
+
     swap.wait_send()
+    for d in range(1, experts):
+        prob_copy(lax.rem(mine + d, experts), mine).wait_send()
     for b in range(chips):
 
         @pl.when(has_up & (z >= b))
@@ -590,7 +685,7 @@
             cross(b, lax.rem(mine + d, experts), mine).wait_send()
 
 
-def expert_return(pre_grad, gate_up, pick, gates, chips, experts):
+def expert_return(pre_grad, gate_up, pick, gates, prob, chips, experts):
     slots, pre_width = pre_grad.shape
     capacity = slots // experts
     shard = gate_up.shape[0]
@@ -601,17 +696,23 @@
     dma = pltpu.SemaphoreType.DMA
     return pl.pallas_call(
         functools.partial(return_kernel, chips, experts),
-        in_specs=[vmem] * 4,
-        out_specs=vmem,
-        out_shape=jax.ShapeDtypeStruct((tok_rows, chips * columns), low),
+        in_specs=[vmem, pl.BlockSpec(memory_space=pl.ANY), vmem, vmem, vmem],
+        out_specs=[vmem, vmem],
+        out_shape=[
+            jax.ShapeDtypeStruct((tok_rows, chips * columns), low),
+            jax.ShapeDtypeStruct((tok_rows, prob.shape[2]), low),
+        ],
         scratch_shapes=[
+            pltpu.VMEM(prob.shape, low),
             pltpu.VMEM((chips, slots, pre_width), low),
             pltpu.VMEM((2, shard, pre_width), low),
             pltpu.VMEM((chips, experts, capacity, columns), low),
             pltpu.VMEM((chips, experts, capacity, columns), low),
             pltpu.VMEM((chips, tok_rows, columns), low),
             pltpu.VMEM((chips, tok_rows, columns), low),
-            dma((2,)),
+            dma((3,)),
+            dma((experts,)),
+            dma((experts,)),
             dma((chips,)),
             dma((chips,)),
             dma((chips,)),
@@ -628,7 +729,7 @@
             bytes_accessed=4 * (slots * pre_width + shard * pre_width),
             transcendentals=0,
         ),
-    )(pre_grad, gate_up, pick, gates)
+    )(pre_grad, gate_up, pick, gates, prob)
 
 
 def body(
@@ -646,71 +747,33 @@
     experts = lax.axis_size("exp")
     contexts = lax.axis_size("ctx")
     tok_rows = grad_out.shape[1]
-    width = grad_out.shape[2]
     filled = saved_pre.shape[2] // experts
     capacity = -(-filled // 16) * 16
     hidden = down_weight.shape[1]
     chips = contexts // 2
 
-    route_rows = routes[0]
-    one_hot = (
-        route_rows.reshape(-1)[:, None] == jnp.arange(experts, dtype=jnp.int32)[None, :]
-    ).astype(jnp.int32)
-    earlier = jnp.cumsum(one_hot, axis=0) - one_hot
-    positions = jnp.sum(earlier * one_hot, axis=-1)
-    slot_keys = route_rows[:, 0] * capacity + positions
-    slots = experts * capacity
-
-    kv_local = keys_values[0]
-    kv_width = kv_local.shape[1]
-    extra = jnp.broadcast_to(
-        jnp.pad(slot_keys.astype(jnp.bfloat16), (0, kv_width - tok_rows))[None], (16, kv_width)
-    )
-    kv_wide = jnp.concatenate([kv_local, extra], axis=0)
-
-    dispatch = (jnp.arange(slots, dtype=jnp.int32)[:, None] == slot_keys[None, :]).astype(
-        jnp.bfloat16
-    )
-    send_rows = jnp.dot(dispatch, grad_out[0], preferred_element_type=jnp.float32).astype(
-        jnp.bfloat16
-    )
-    query_grad, kv_grad, down_grad, block_extra = gather_and_attend(
-        kv_wide,
+    pre_acts = saved_pre[0, 0]
+    if capacity != filled:
+        pre_acts = pre_acts.reshape(experts, filled, 2 * hidden)
+        pre_acts = jnp.pad(pre_acts, ((0, 0), (0, capacity - filled), (0, 0)))
+        pre_acts = pre_acts.reshape(experts * capacity, 2 * hidden)
+    query_grad, kv_grad, pre_grad, prob, pick = gather_and_attend(
+        routes.reshape(1, tok_rows),
+        keys_values[0],
         down_weight[0],
-        send_rows.reshape(experts, capacity, width),
+        grad_out[0],
+        pre_acts,
         queries[0],
         attn_grad[0],
         attn_out[0],
         chips,
+        experts,
     )
-    block_keys = block_extra[:, 0, :tok_rows].astype(jnp.int32)
-
-    pre_acts = saved_pre[0, 0]
-    if capacity != filled:
-        pre_acts = pre_acts.reshape(experts, filled, 2 * hidden)
-        pre_acts = jnp.pad(pre_acts, ((0, 0), (0, capacity - filled), (0, 0)))
-        pre_acts = pre_acts.reshape(slots, 2 * hidden)
-    gate_pre = pre_acts[:, :hidden].astype(jnp.float32)
-    up_pre = pre_acts[:, hidden:].astype(jnp.float32)
-    sigma = jax.nn.sigmoid(gate_pre)
-    swish = gate_pre * sigma
-    slot_prob = jnp.sum(down_grad * swish * up_pre, axis=-1).astype(jnp.bfloat16)
-    gate_part = down_grad * up_pre * sigma * (1.0 + gate_pre * (1.0 - sigma))
-    up_part = down_grad * swish
-    pre_grad = jnp.concatenate([gate_part, up_part], axis=-1).astype(jnp.bfloat16)
-
-    back_prob = lax.all_to_all(
-        slot_prob.reshape(experts, capacity), "exp", split_axis=0, concat_axis=0, tiled=True
-    ).reshape(slots)
-    pick = (block_keys[:, :, None] == jnp.arange(slots, dtype=jnp.int32)).astype(jnp.bfloat16)
-    moe_input_grad = expert_return(
-        pre_grad, gate_up_weight[0], pick, gate_probs[0], chips, experts
-    )[None]
-    own_slots = slot_keys[:, None] == jnp.arange(slots, dtype=jnp.int32)
-    prob_grad = jnp.sum(
-        jnp.where(own_slots, back_prob.astype(jnp.float32), 0.0), axis=1
-    ).astype(jnp.bfloat16)[None, :, None]
-    return (moe_input_grad, prob_grad, query_grad[None], kv_grad[None])
+    moe_input_grad, token_prob = expert_return(
+        pre_grad, gate_up_weight[0], pick, gate_probs[0], prob, chips, experts
+    )
+    prob_grad = token_prob[:, :1][None]
+    return (moe_input_grad[None], prob_grad, query_grad[None], kv_grad[None])
 
 
 def solution(mesh):

time: 162 us -> 152 us (0.938)
  other arithmetic: 3.81 us -> 0 us
  starting transfers between devices: 3.53 us -> 0 us
  Pallas kernels: 147 us -> 145 us
  local copies, waits for them, and re-layouts: 4.91 us -> 6.85 us
  matrix products: 1.72 us -> 0 us
    all_to_all x1 -> x0, starting transfers between devices: 3.53 us -> none  [body(): lax.all_to_all(slot_prob.reshape(experts, capacity), 'exp', split_axis=0,...]
    pallas_call x1, Pallas kernels: 83.1 us -> 80.9 us  [gather_and_attend(): pl.pallas_call(functools.partial(gather_kernel, chips, experts), in_specs...]
    reduce_sum x3 -> x0, other arithmetic: 1.93 us -> none  [the longest x1 0.88 us: body(): positions = jnp.sum(earlier * one_hot, axis=-1)]
    dot_general x1 -> x0, matrix products: 1.72 us -> none  [body(): jnp.dot(dispatch, grad_out[0], preferred_element_type=jnp.float32)]
    convert_element_type x5 -> x0, other arithmetic: 1.66 us -> none  [the longest x1 0.83 us: body(): one_hot = (route_rows.reshape(-1)[:, None] == jnp.arange(experts, dtype=j...]
    unnamed x17 -> x15, local copies, waits for them, and re-layouts: 4.03 us -> 5.46 us
  transfers between devices with their start and end apart: 1 -> 0, of which waited for: 0 -> 0; matrix products, arithmetic and copies ran while one was open for 0% -> 0% of each run, Pallas kernels for 39% -> 0%
where the time goes in v5:
time: 152 us
  Pallas kernels  145 us (95%)
  local copies, waits for them, and re-layouts  6.85 us (5%)
    pallas_call x1, Pallas kernels, gather_and_attend(): pl.pallas_call(functools.partial(gather_kernel, chips, experts), in_specs...  80.9 us
    pallas_call x1, Pallas kernels, expert_return(): pl.pallas_call(functools.partial(return_kernel, chips, experts), in_specs...  63.7 us
    unnamed x15, local copies, waits for them, and re-layouts  5.46 us

profile of v5, /device:TPU:0, one launch (start us, length us, event | category | flops | bytes accessed | tf_op | source)
XLA Modules:
  0.0 152.1 jit_solution(4411490342928111822)
XLA Ops:
  0.6 0.8 copy.15.gate_ref
  1.4 0.0 copy-start
  1.4 80.9 %shard_map.129 = (bf16[128,4096]{1,0:T(8,128)(2,1)}, bf16[128,512]{1,0:T(8,128)(2,1)}, bf16[192,1536]{1,0:T(8,128)(2,1)}, bf16[4,48,128]{2,1,0:T(8,128)(2,1)}, bf16[4,128,192]{2,1,0:T(8,128)(2,1)}) custom-call(s32[1,128]{1,0:T(1,128)} %bitcast.27, bf16[128,512]{1,0:T(8,128)(2,1)} %bitcast.26, bf16[768,512]{1,0:T(8,128)(2,1)} %bitcast.24, ...), custom_call_target="tpu_custom_call" | custom-call | flops 5368709120 | bytes 4194304 | tf_op jit(solution)/shard_map/pallas_call | solution.py:426
  82.3 0.0 copy-done
  82.3 0.0 copy-start.1
  82.3 1.1 copy-done.1
  83.4 0.0 copy-start.2
  83.4 0.9 copy-done.2
  84.3 0.0 copy-start.3
  84.3 0.8 copy-done.3
  85.1 63.7 %shard_map.130 = (bf16[128,4096]{1,0:T(8,128)(2,1)S(1)}, bf16[128,128]{1,0:T(8,128)(2,1)S(1)}) custom-call(bf16[192,1536]{1,0:T(8,128)(2,1)S(1)} %copy-done.1, bf16[512,1536]{1,0:T(8,128)(2,1)S(1)} %bitcast.15, bf16[4,128,192]{2,1,0:T(8,128)(2,1)S(1)} %copy-done.2, f32[128,1]{1,0:T(8,128)S(1)} %copy.15.gate_ref, bf16[4,48,128]{2,1,0:T(8,128)(2,1)S(1)} %copy-done.3), custom_call_target="tpu_custom_call" | custom-call | flops 2415919104 | bytes 4325376 | tf_op jit(solution)/shard_map/pallas_call | solution.py:697
  148.8 0.0 copy-start.4
  148.9 0.6 slice_reduce_fusion
  149.5 1.0 copy.19
  150.5 0.0 copy-done.4
  150.5 0.0 copy-start.5
  150.5 1.0 copy.20
  151.4 0.1 copy-done.5
  151.5 0.7 copy.21
Async XLA Ops:
  1.4 80.9 %copy-start = (bf16[1,512,1536]{2,1,0:T(8,128)(2,1)S(1)}, bf16[1,512,1536]{2,1,0:T(8,128)(2,1)}, u32[]{:S(2)}) copy-start(bf16[1,512,1536]{2,1,0:T(8,128)(2,1)} %param.15) | copy-start | bytes 4718596
  82.3 1.1 copy-start.1
  83.4 0.9 copy-start.2
  84.3 0.8 copy-start.3
  148.8 1.6 %copy-start.4 = (bf16[128,4096]{1,0:T(8,128)(2,1)S(1)}, bf16[128,4096]{1,0:T(8,128)(2,1)}, u32[]{:S(2)}) copy-start(bf16[128,4096]{1,0:T(8,128)(2,1)} %get-tuple-element.16) | copy-start | bytes 3145732
  150.5 1.0 copy-start.5

commit v6 on v5

--- a/solution.py
+++ b/solution.py
@@ -17,7 +17,219 @@
 MESH = pl.DeviceIdType.MESH
 
 
-def gather_kernel(
+def return_parts(
+    chips,
+    experts,
+    gu_ref,
+    pick_ref,
+    gate_ref,
+    prob_ref,
+    out_ref,
+    token_prob_ref,
+    prob_buf,
+    pre_buf,
+    gu_buf,
+    sent,
+    came,
+    leaving,
+    landed,
+    pair_sems,
+    prob_out,
+    prob_in,
+    up_sems,
+    down_sems,
+    pre_sems,
+    cross_out,
+    cross_in,
+    back_out,
+    back_in,
+):
+    me = lax.axis_index("ctx")
+    mine = lax.axis_index("exp")
+    z = lax.div(me, 2)
+    core = lax.rem(me, 2)
+    shard = gu_ref.shape[0]
+    columns = 2 * shard
+    tile = min(shard, 256)
+
+    other = 2 * z + 1 - core
+
+    def remote(src, dst, send, recv, device):
+        return pltpu.make_async_remote_copy(
+            src_ref=src,
+            dst_ref=dst,
+            send_sem=send,
+            recv_sem=recv,
+            device_id=device,
+            device_id_type=MESH,
+        )
+
+    def up(b):
+        return remote(
+            pre_buf.at[b], pre_buf.at[b], up_sems.at[b], pre_sems.at[b], {"ctx": me + 2}
+        )
+
+    def down(b):
+        return remote(
+            pre_buf.at[b], pre_buf.at[b], down_sems.at[b], pre_sems.at[b], {"ctx": me - 2}
+        )
+
+    def cross(b, to, slot):
+        return remote(
+            sent.at[b, to], came.at[b, slot], cross_out.at[b, to], cross_in.at[b, slot], {"exp": to}
+        )
+
+    def back(b, slot):
+        return remote(
+            leaving.at[b],
+            landed.at[slot],
+            back_out.at[b],
+            back_in.at[slot],
+            {"ctx": 2 * b + core},
+        )
+
+    swap = remote(
+        gu_ref, gu_buf.at[core], pair_sems.at[0], pair_sems.at[1], {"ctx": other}
+    )
+    has_up = z + 1 < chips
+    has_down = z > 0
+
+    def prob_copy(to, slot):
+        return remote(
+            prob_ref.at[to], prob_buf.at[slot], prob_out.at[to], prob_in.at[slot], {"exp": to}
+        )
+
+    def block_of(i):
+        ahead = lax.rem(z + i, chips)
+        behind = lax.rem(z - i + chips, chips)
+        return jnp.where(z < chips // 2, ahead, behind)
+
+    def combine(b):
+        for d in range(1, experts):
+            j = lax.rem(mine + d, experts)
+            cross(b, j, j).wait_recv()
+        slots = pick_ref.shape[2]
+        for t in range(columns // tile):
+            cols = pl.ds(t * tile, tile)
+            rows = came[b, :, :, cols].reshape(slots, tile)
+            leaving[b, :, cols] = jnp.dot(
+                pick_ref[b], rows, preferred_element_type=jnp.float32
+            ).astype(leaving.dtype)
+
+        @pl.when(b != z)
+        def _():
+            back(b, z).start()
+
+        @pl.when(b == z)
+        def _():
+            landed[z] = leaving[b]
+
+    def turn(i, carry):
+        lo = z - i
+        hi = z + i
+
+        @pl.when((i > 0) & (lo >= 0))
+        def _():
+            up(lo).wait_recv()
+
+            @pl.when(has_up)
+            def _():
+                up(lo).start()
+
+        @pl.when((i > 0) & (hi < chips))
+        def _():
+            down(hi).wait_recv()
+
+            @pl.when(has_down)
+            def _():
+                down(hi).start()
+
+        b = block_of(i)
+        for half in range(2):
+            for t in range(shard // tile):
+                weights = gu_buf[half, pl.ds(t * tile, tile), :]
+                grads = lax.dot_general(
+                    pre_buf[b], weights, NT, preferred_element_type=jnp.float32
+                )
+                cols = pl.ds(half * shard + t * tile, tile)
+                sent[b, :, :, cols] = grads.astype(sent.dtype).reshape(experts, -1, tile)
+        for d in range(1, experts):
+            cross(b, lax.rem(mine + d, experts), mine).start()
+        came[b, mine] = sent[b, mine]
+
+        @pl.when(i > 0)
+        def _():
+            combine(block_of(i - 1))
+
+        return carry
+
+    keep = pltpu.make_async_copy(gu_ref, gu_buf.at[core], pair_sems.at[2])
+
+    def early():
+        swap.start()
+        keep.start()
+
+    def run():
+        @pl.when(has_up)
+        def _():
+            up(z).start()
+
+        @pl.when(has_down)
+        def _():
+            down(z).start()
+
+        for d in range(1, experts):
+            prob_copy(lax.rem(mine + d, experts), mine).start()
+        prob_buf[mine] = prob_ref[mine]
+        keep.wait()
+        swap.wait_recv()
+
+        lax.fori_loop(0, chips, turn, 0)
+        combine(block_of(chips - 1))
+        for b in range(chips):
+
+            @pl.when(z != b)
+            def _():
+                back(b, b).wait_recv()
+
+            out_ref[:, pl.ds(b * columns, columns)] = (
+                gate_ref[...] * landed[b].astype(jnp.float32)
+            ).astype(out_ref.dtype)
+
+        for d in range(1, experts):
+            j = lax.rem(mine + d, experts)
+            prob_copy(j, j).wait_recv()
+        lanes = prob_ref.shape[2]
+        token_prob_ref[...] = jnp.dot(
+            pick_ref[z],
+            prob_buf[...].reshape(pick_ref.shape[2], lanes),
+            preferred_element_type=jnp.float32,
+        ).astype(token_prob_ref.dtype)
+
+        swap.wait_send()
+        for d in range(1, experts):
+            prob_copy(lax.rem(mine + d, experts), mine).wait_send()
+        for b in range(chips):
+
+            @pl.when(has_up & (z >= b))
+            def _():
+                up(b).wait_send()
+
+            @pl.when(has_down & (z <= b))
+            def _():
+                down(b).wait_send()
+
+            @pl.when(z != b)
+            def _():
+                back(b, z).wait_send()
+
+            for d in range(1, experts):
+                cross(b, lax.rem(mine + d, experts), mine).wait_send()
+
+    return early, run
+
+
+def layer_kernel(
     chips,
     experts,
     routes_ref,
@@ -28,9 +240,12 @@
     q_ref,
     g_ref,
     o_ref,
+    gate_ref,
+    gu_ref,
     dq_ref,
     kv_grad_ref,
-    pre_ref,
+    out_ref,
+    token_prob_ref,
     prob_ref,
     pick_ref,
     rows_ref,
@@ -63,6 +278,9 @@
     pair_in,
     term_out,
     term_in,
+    prob_buf,
+    pre_buf,
+    *return_refs,
 ):
     me = lax.axis_index("ctx")
     mine = lax.axis_index("exp")
@@ -201,8 +419,22 @@
             rows_ref.at[to], row_buf.at[slot], row_out.at[to], row_in.at[slot], {"exp": to}
         )
 
+    early, run = return_parts(
+        chips,
+        experts,
+        gu_ref,
+        pick_ref,
+        gate_ref,
+        prob_ref,
+        out_ref,
+        token_prob_ref,
+        prob_buf,
+        pre_buf,
+        *return_refs,
+    )
     kv_line.begin()
     w_line.begin()
+    early()
     dispatch = one_hot(slot_keys).astype(jnp.bfloat16)
     wide = 512
     for t in range(width // wide):
@@ -375,13 +607,14 @@
             up_part = grad * swish
             prob = prob + jnp.sum(up_part * up_pre, axis=-1, keepdims=True)
             gate_part = grad * up_pre * sigma * (1.0 + gate_pre * (1.0 - sigma))
-            pre_ref[:, t : t + tile] = gate_part.astype(pre_ref.dtype)
-            pre_ref[:, hidden + t : hidden + t + tile] = up_part.astype(pre_ref.dtype)
+            pre_buf[z, :, t : t + tile] = gate_part.astype(pre_buf.dtype)
+            pre_buf[z, :, hidden + t : hidden + t + tile] = up_part.astype(pre_buf.dtype)
     prob_ref[...] = (
         jnp.broadcast_to(prob, (slots, prob_ref.shape[2]))
         .astype(prob_ref.dtype)
         .reshape(prob_ref.shape)
     )
+    run()
 
     landed_sum = terms[rows_of(z, core), :] + pair_terms[z]
     kv_sum = pair_terms.at[z]
@@ -410,7 +643,9 @@
             term_copy(b, z).wait_send()
 
 
-def gather_and_attend(routes, kv_local, down, tokens, acts, q, g, o, chips, experts):
+def layer_backward(
+    routes, kv_local, down, tokens, acts, q, g, o, gates, gate_up, chips, experts
+):
     tok_rows, width = q.shape
     kv_width = kv_local.shape[1]
     seq_len = 2 * chips * tok_rows
@@ -424,17 +659,18 @@
     dma = pltpu.SemaphoreType.DMA
     per_chip = dma((chips,))
     return pl.pallas_call(
-        functools.partial(gather_kernel, chips, experts),
-        in_specs=[vmem] * 8,
-        out_specs=[vmem] * 5,
+        functools.partial(layer_kernel, chips, experts),
+        in_specs=[vmem] * 9 + [pl.BlockSpec(memory_space=pl.ANY)],
+        out_specs=[vmem] * 4,
         out_shape=[
             jax.ShapeDtypeStruct((tok_rows, width), low),
             jax.ShapeDtypeStruct((tok_rows, kv_width), low),
-            jax.ShapeDtypeStruct((slots, 2 * hidden), low),
-            jax.ShapeDtypeStruct((experts, capacity, 128), low),
-            jax.ShapeDtypeStruct((chips, tok_rows, slots), low),
+            jax.ShapeDtypeStruct((tok_rows, width), low),
+            jax.ShapeDtypeStruct((tok_rows, 128), low),
         ],
         scratch_shapes=[
+            pltpu.VMEM((experts, capacity, 128), low),
+            pltpu.VMEM((chips, tok_rows, slots), low),
             pltpu.VMEM((experts, capacity, width), low),
             pltpu.VMEM((slots, hidden), full),
             pltpu.VMEM((chips, 2, tok_rows + 16, kv_width), low),
@@ -453,283 +689,35 @@
         + [dma((chips, 1))] * 5
         + [dma((chips, PARTS))] * 5
         + [dma((experts,))] * 2
-        + [per_chip] * 4,
+        + [per_chip] * 4
+        + [
+            pltpu.VMEM((experts, capacity, 128), low),
+            pltpu.VMEM((chips, slots, 2 * hidden), low),
+            pltpu.VMEM((2, shard, 2 * hidden), low),
+            pltpu.VMEM((chips, experts, capacity, 2 * shard), low),
+            pltpu.VMEM((chips, experts, capacity, 2 * shard), low),
+            pltpu.VMEM((chips, tok_rows, 2 * shard), low),
+            pltpu.VMEM((chips, tok_rows, 2 * shard), low),
+            dma((3,)),
+            dma((experts,)),
+            dma((experts,)),
+            per_chip,
+            per_chip,
+            per_chip,
+            dma((chips, experts)),
+            dma((chips, experts)),
+            per_chip,
+            per_chip,
+        ],
         compiler_params=pltpu.CompilerParams(
-            collective_id=1, has_side_effects=True, vmem_limit_bytes=54 * 1024 * 1024
+            collective_id=0, has_side_effects=True, vmem_limit_bytes=60 * 1024 * 1024
         ),
         cost_estimate=pl.CostEstimate(
             flops=10 * tok_rows * seq_len * width,
             bytes_accessed=8 * tok_rows * width,
             transcendentals=tok_rows * seq_len * width // hd,
         ),
-    )(routes, kv_local, down, tokens, acts, q, g, o)
-
-
-def return_kernel(
-    chips,
-    experts,
-    pre_ref,
-    gu_ref,
-    pick_ref,
-    gate_ref,
-    prob_ref,
-    out_ref,
-    token_prob_ref,
-    prob_buf,
-    pre_buf,
-    gu_buf,
-    sent,
-    came,
-    leaving,
-    landed,
-    pair_sems,
-    prob_out,
-    prob_in,
-    up_sems,
-    down_sems,
-    pre_sems,
-    cross_out,
-    cross_in,
-    back_out,
-    back_in,
-):
-    me = lax.axis_index("ctx")
-    mine = lax.axis_index("exp")
-    z = lax.div(me, 2)
-    core = lax.rem(me, 2)
-    shard = gu_ref.shape[0]
-    columns = 2 * shard
-    tile = min(shard, 256)
-
-    barrier = pltpu.get_barrier_semaphore()
-    for d in range(1, chips):
-        chip = lax.rem(z + d, chips)
-        pl.semaphore_signal(
-            barrier, inc=1, device_id={"ctx": 2 * chip + core}, device_id_type=MESH
-        )
-    for d in range(1, experts):
-        pl.semaphore_signal(
-            barrier, inc=1, device_id={"exp": lax.rem(mine + d, experts)}, device_id_type=MESH
-        )
-    other = 2 * z + 1 - core
-    pl.semaphore_signal(barrier, inc=1, device_id={"ctx": other}, device_id_type=MESH)
-    pre_buf[z] = pre_ref[...]
-    pl.semaphore_wait(barrier, chips + experts - 1)
-
-    def remote(src, dst, send, recv, device):
-        return pltpu.make_async_remote_copy(
-            src_ref=src,
-            dst_ref=dst,
-            send_sem=send,
-            recv_sem=recv,
-            device_id=device,
-            device_id_type=MESH,
-        )
-
-    def up(b):
-        return remote(
-            pre_buf.at[b], pre_buf.at[b], up_sems.at[b], pre_sems.at[b], {"ctx": me + 2}
-        )
-
-    def down(b):
-        return remote(
-            pre_buf.at[b], pre_buf.at[b], down_sems.at[b], pre_sems.at[b], {"ctx": me - 2}
-        )
-
-    def cross(b, to, slot):
-        return remote(
-            sent.at[b, to], came.at[b, slot], cross_out.at[b, to], cross_in.at[b, slot], {"exp": to}
-        )
-
-    def back(b, slot):
-        return remote(
-            leaving.at[b],
-            landed.at[slot],
-            back_out.at[b],
-            back_in.at[slot],
-            {"ctx": 2 * b + core},
-        )
-
-    swap = remote(
-        gu_ref, gu_buf.at[core], pair_sems.at[0], pair_sems.at[1], {"ctx": other}
-    )
-    has_up = z + 1 < chips
-    has_down = z > 0
-
-    @pl.when(has_up)
-    def _():
-        up(z).start()
-
-    @pl.when(has_down)
-    def _():
-        down(z).start()
-
-    def prob_copy(to, slot):
-        return remote(
-            prob_ref.at[to], prob_buf.at[slot], prob_out.at[to], prob_in.at[slot], {"exp": to}
-        )
-
-    swap.start()
-    keep = pltpu.make_async_copy(gu_ref, gu_buf.at[core], pair_sems.at[2])
-    keep.start()
-    for d in range(1, experts):
-        prob_copy(lax.rem(mine + d, experts), mine).start()
-    prob_buf[mine] = prob_ref[mine]
-    keep.wait()
-    swap.wait_recv()
-
-    def block_of(i):
-        ahead = lax.rem(z + i, chips)
-        behind = lax.rem(z - i + chips, chips)
-        return jnp.where(z < chips // 2, ahead, behind)
-
-    def combine(b):
-        for d in range(1, experts):
-            j = lax.rem(mine + d, experts)
-            cross(b, j, j).wait_recv()
-        slots = pick_ref.shape[2]
-        for t in range(columns // tile):
-            cols = pl.ds(t * tile, tile)
-            rows = came[b, :, :, cols].reshape(slots, tile)
-            leaving[b, :, cols] = jnp.dot(
-                pick_ref[b], rows, preferred_element_type=jnp.float32
-            ).astype(leaving.dtype)
-
-        @pl.when(b != z)
-        def _():
-            back(b, z).start()
-
-        @pl.when(b == z)
-        def _():
-            landed[z] = leaving[b]
-
-    def turn(i, carry):
-        lo = z - i
-        hi = z + i
-
-        @pl.when((i > 0) & (lo >= 0))
-        def _():
-            up(lo).wait_recv()
-
-            @pl.when(has_up)
-            def _():
-                up(lo).start()
-
-        @pl.when((i > 0) & (hi < chips))
-        def _():
-            down(hi).wait_recv()
-
-            @pl.when(has_down)
-            def _():
-                down(hi).start()
-
-        b = block_of(i)
-        for half in range(2):
-            for t in range(shard // tile):
-                weights = gu_buf[half, pl.ds(t * tile, tile), :]
-                grads = lax.dot_general(
-                    pre_buf[b], weights, NT, preferred_element_type=jnp.float32
-                )
-                cols = pl.ds(half * shard + t * tile, tile)
-                sent[b, :, :, cols] = grads.astype(sent.dtype).reshape(experts, -1, tile)
-        for d in range(1, experts):
-            cross(b, lax.rem(mine + d, experts), mine).start()
-        came[b, mine] = sent[b, mine]
-
-        @pl.when(i > 0)
-        def _():
-            combine(block_of(i - 1))
-
-        return carry
-
-    lax.fori_loop(0, chips, turn, 0)
-    combine(block_of(chips - 1))
-    for b in range(chips):
-
-        @pl.when(z != b)
-        def _():
-            back(b, b).wait_recv()
-
-        out_ref[:, pl.ds(b * columns, columns)] = (
-            gate_ref[...] * landed[b].astype(jnp.float32)
-        ).astype(out_ref.dtype)
-
-    for d in range(1, experts):
-        j = lax.rem(mine + d, experts)
-        prob_copy(j, j).wait_recv()
-    lanes = prob_ref.shape[2]
-    token_prob_ref[...] = jnp.dot(
-        pick_ref[z],
-        prob_buf[...].reshape(pick_ref.shape[2], lanes),
-        preferred_element_type=jnp.float32,
-    ).astype(token_prob_ref.dtype)
-
-    swap.wait_send()
-    for d in range(1, experts):
-        prob_copy(lax.rem(mine + d, experts), mine).wait_send()
-    for b in range(chips):
-
-        @pl.when(has_up & (z >= b))
-        def _():
-            up(b).wait_send()
-
-        @pl.when(has_down & (z <= b))
-        def _():
-            down(b).wait_send()
-
-        @pl.when(z != b)
-        def _():
-            back(b, z).wait_send()
-
-        for d in range(1, experts):
-            cross(b, lax.rem(mine + d, experts), mine).wait_send()
-
-
-def expert_return(pre_grad, gate_up, pick, gates, prob, chips, experts):
-    slots, pre_width = pre_grad.shape
-    capacity = slots // experts
-    shard = gate_up.shape[0]
-    tok_rows = gates.shape[0]
-    columns = 2 * shard
-    vmem = pl.BlockSpec(memory_space=pltpu.VMEM)
-    low = jnp.bfloat16
-    dma = pltpu.SemaphoreType.DMA
-    return pl.pallas_call(
-        functools.partial(return_kernel, chips, experts),
-        in_specs=[vmem, pl.BlockSpec(memory_space=pl.ANY), vmem, vmem, vmem],
-        out_specs=[vmem, vmem],
-        out_shape=[
-            jax.ShapeDtypeStruct((tok_rows, chips * columns), low),
-            jax.ShapeDtypeStruct((tok_rows, prob.shape[2]), low),
-        ],
-        scratch_shapes=[
-            pltpu.VMEM(prob.shape, low),
-            pltpu.VMEM((chips, slots, pre_width), low),
-            pltpu.VMEM((2, shard, pre_width), low),
-            pltpu.VMEM((chips, experts, capacity, columns), low),
-            pltpu.VMEM((chips, experts, capacity, columns), low),
-            pltpu.VMEM((chips, tok_rows, columns), low),
-            pltpu.VMEM((chips, tok_rows, columns), low),
-            dma((3,)),
-            dma((experts,)),
-            dma((experts,)),
-            dma((chips,)),
-            dma((chips,)),
-            dma((chips,)),
-            dma((chips, experts)),
-            dma((chips, experts)),
-            dma((chips,)),
-            dma((chips,)),
-        ],
-        compiler_params=pltpu.CompilerParams(
-            collective_id=0, has_side_effects=True, vmem_limit_bytes=40 * 1024 * 1024
-        ),
-        cost_estimate=pl.CostEstimate(
-            flops=2 * chips * slots * pre_width * columns,
-            bytes_accessed=4 * (slots * pre_width + shard * pre_width),
-            transcendentals=0,
-        ),
-    )(pre_grad, gate_up, pick, gates, prob)
+    )(routes, kv_local, down, tokens, acts, q, g, o, gates, gate_up)
 
 
 def body(
@@ -757,7 +745,7 @@
         pre_acts = pre_acts.reshape(experts, filled, 2 * hidden)
         pre_acts = jnp.pad(pre_acts, ((0, 0), (0, capacity - filled), (0, 0)))
         pre_acts = pre_acts.reshape(experts * capacity, 2 * hidden)
-    query_grad, kv_grad, pre_grad, prob, pick = gather_and_attend(
+    query_grad, kv_grad, moe_input_grad, token_prob = layer_backward(
         routes.reshape(1, tok_rows),
         keys_values[0],
         down_weight[0],
@@ -766,11 +754,10 @@
         queries[0],
         attn_grad[0],
         attn_out[0],
+        gate_probs[0],
+        gate_up_weight[0],
         chips,
         experts,
-    )
-    moe_input_grad, token_prob = expert_return(
-        pre_grad, gate_up_weight[0], pick, gate_probs[0], prob, chips, experts
     )
     prob_grad = token_prob[:, :1][None]
     return (moe_input_grad[None], prob_grad, query_grad[None], kv_grad[None])

time: 152 us -> 153 us (level)
    unnamed x15 -> x7, local copies, waits for them, and re-layouts: 5.46 us -> 3.97 us
    pallas_call x2 -> x1, Pallas kernels: 145 us -> 145 us  [layer_backward(): pl.pallas_call(functools.partial(layer_kernel, chips, experts), in_specs=...]
where the time goes in v6:
time: 153 us
  Pallas kernels  145 us (95%)
  local copies, waits for them, and re-layouts  6.83 us (4%)
    pallas_call x1, Pallas kernels, layer_backward(): pl.pallas_call(functools.partial(layer_kernel, chips, experts), in_specs=...  145 us
    unnamed x7, local copies, waits for them, and re-layouts  3.97 us

profile of v6, /device:TPU:0, one launch (start us, length us, event | category | flops | bytes accessed | tf_op | source)
XLA Modules:
  0.0 152.9 jit_solution(11101837556488040005)
XLA Ops:
  0.6 1.4 copy.15.gate_ref
  2.0 145.4 %shard_map.129 = (bf16[128,4096]{1,0:T(8,128)(2,1)}, bf16[128,512]{1,0:T(8,128)(2,1)}, bf16[128,4096]{1,0:T(8,128)(2,1)}, bf16[128,128]{1,0:T(8,128)(2,1)}) custom-call(s32[1,128]{1,0:T(1,128)} %bitcast.27, bf16[128,512]{1,0:T(8,128)(2,1)} %bitcast.26, bf16[768,512]{1,0:T(8,128)(2,1)} %bitcast.24, bf16[128,4096]{1,0:T(8,128)(2,1)} %bitcast.20, ...), custom_call_target="tpu_custom_call" | custom-call | flops 5368709120 | bytes 4194304 | tf_op jit(solution)/shard_map/pallas_call | solution.py:661
  147.4 0.0 copy-start
  147.4 1.5 slice_reduce_fusion
  148.9 2.3 %copy.19 = bf16[1,128,4096]{2,1,0:T(8,128)(2,1)} copy(bf16[1,128,4096]{2,1,0:T(8,128)(2,1)} %bitcast.15) | data formatting | bytes 2097152
  151.2 0.0 copy-done
  151.2 0.0 copy-start.1
  151.2 1.0 copy.20
  152.2 0.1 copy-done.1
  152.2 0.7 copy.21
Async XLA Ops:
  147.4 3.8 %copy-start = (bf16[128,4096]{1,0:T(8,128)(2,1)S(1)}, bf16[128,4096]{1,0:T(8,128)(2,1)}, u32[]{:S(2)}) copy-start(bf16[128,4096]{1,0:T(8,128)(2,1)} %get-tuple-element.10) | copy-start | bytes 3145732
  151.2 1.0 copy-start.1
